TPU v7x, 256 devices: a whole 4x4x8 slice. The times are simulated.
256 devices in a mesh: seq: 64 (over z, x, core), head: 4 (over y).
Axes of the slice: x: 4, y: 4, z: 8, core: 2. Of those that a mesh axis runs over, the one named last changes fastest.
Arguments:
- video_q: bfloat16 [8192, 2048], P('seq', 'head'), may hold values from -7.5 to 7.5
- video_k: bfloat16 [8192, 2048], P('seq', 'head'), may hold values from -7.5 to 7.5
- video_v: bfloat16 [8192, 2048], P('seq', 'head'), may hold values from -24 to 24
- audio_q: bfloat16 [512, 2048], P('seq', 'head'), may hold values from -7.5 to 7.5
- audio_k: bfloat16 [512, 2048], P('seq', 'head'), may hold values from -7.5 to 7.5
- audio_v: bfloat16 [512, 2048], P('seq', 'head'), may hold values from -24 to 24
- video_lengths: int32 [4], replicated, may hold values from 1 to 3584, 8192 in all
- audio_lengths: int32 [4], replicated, may hold values from 1 to 224, 512 in all
- video_out_weight: bfloat16 [2048, 4096], P(None, 'head'), may hold values from -0.125 to 0.125
- audio_out_weight: bfloat16 [2048, 2048], P(None, 'head'), may hold values from -0.125 to 0.125
Outputs:
- video_out: bfloat16 [8192, 4096], P('seq', 'head')
- audio_out: bfloat16 [512, 2048], P('seq', 'head')
Inputs may be any that keep to these rules, and one draw needn't show every extreme that they name: `video_lengths`: clips lie end to end in order; one clip has exactly 3584 video tokens. `audio_lengths`: clips lie end to end in order; one clip has exactly 224 audio tokens.
All inputs are finite; a program needn't handle non-finite values.
Results may differ from a plain program's by a relative error of at most 0.012.
Values may be sent and summed in bfloat16 or wider, within the bound.
A program may use at most 64 MiB of HBM per device.

v0:
```python
import math

import jax
import jax.numpy as jnp
from jax import lax
from jax.sharding import Mesh
from jax.sharding import PartitionSpec as P

HEAD_DIM = 64
SEQ = ("seq_0", "seq_1", "seq_2")


masked_floor = -1e30


def sent_to_all(value, axis):
    count = lax.axis_size(axis)
    return lax.all_to_all(
        jnp.broadcast_to(value[None], (count, *value.shape)), axis, 0, 0, tiled=True
    )


def in_order(pieces, dim):
    pieces = jnp.moveaxis(pieces, 0, dim)
    dims = pieces.shape
    return pieces.reshape(*dims[:dim], dims[dim] * dims[dim + 1], *dims[dim + 2 :])


def gather_axes(value, axes, dim):
    far, near = axes
    first = sent_to_all(value, far)
    pieces = jnp.swapaxes(sent_to_all(first, near), 0, 1)
    return in_order(pieces.reshape(-1, *value.shape), dim)


def sent_together(arrays, axis, dim, along):
    both = jnp.concatenate(arrays, axis=along)
    filled, at, finished = (gather_axes(both, axis, dim), 0, [])
    for a in arrays:
        finished.append(lax.slice_in_dim(filled, at, at + a.shape[along], axis=along))
        at += a.shape[along]
    return tuple(finished)


def taken_together(value, axis):
    return sent_to_all(value, axis).max(axis=0)


def in_blocks(value, dim, count):
    dims = value.shape
    pieces = value.reshape(*dims[:dim], count, dims[dim] // count, *dims[dim + 1 :])
    return jnp.moveaxis(pieces, dim, 0)


def sum_at_owner(value, axis, dim):
    count = lax.axis_size(axis)
    pieces = lax.all_to_all(in_blocks(value, dim, count), axis, 0, 0, tiled=True)
    return jnp.sum(pieces, axis=0)


def sum_by_axis(value, axes, dim):
    far, near = axes
    own = sum_at_owner(in_blocks(value, dim, lax.axis_size(far)), near, dim + 1)
    return jnp.sum(lax.all_to_all(own, far, 0, 0, tiled=True), axis=0)


def sent_together_2(arrays, axis, dim, along):
    both = jnp.concatenate(arrays, axis=along)
    filled, at, finished = (sum_by_axis(both, axis, dim), 0, [])
    for a in arrays:
        finished.append(lax.slice_in_dim(filled, at, at + a.shape[along], axis=along))
        at += a.shape[along]
    return tuple(finished)


def gathered_copies(value, axis, dim):
    pieces = sent_to_all(value, axis)
    return in_order(pieces, dim)


def clip_index(positions, lengths):
    clip_ends = jnp.cumsum(lengths)
    return jnp.sum((positions[:, None] >= clip_ends[None, :]).astype(jnp.int32), axis=1)


def audio_clips(stored, audio_total, lengths):
    positions = (stored + audio_total // 2) % audio_total
    return clip_index(positions, lengths)


def per_device(
    video_q,
    video_k,
    video_v,
    audio_q,
    audio_k,
    audio_v,
    video_lengths,
    audio_lengths,
    video_out_weight,
    audio_out_weight,
):
    seq_count = lax.axis_size(SEQ)
    seq_rank = lax.axis_index(SEQ)
    video_rows, local_width = video_q.shape
    audio_rows = audio_q.shape[0]
    local_heads = local_width // HEAD_DIM
    audio_total = audio_rows * seq_count
    score_scale = 1.0 / math.sqrt(HEAD_DIM)
    video_clip = clip_index(
        seq_rank * video_rows + jnp.arange(video_rows, dtype=jnp.int32), video_lengths
    )
    query_clip = audio_clips(jnp.arange(audio_total, dtype=jnp.int32), audio_total, audio_lengths)
    every_query, every_key, every_value = sent_together(
        (audio_q, audio_k, audio_v), (("seq_0", "seq_1"), "seq_2"), 0, 1
    )
    query_heads = video_q.reshape(video_rows, local_heads, HEAD_DIM)
    scores = (
        jnp.einsum(
            "qhd,khd->qhk",
            query_heads,
            every_key.reshape(audio_total, local_heads, HEAD_DIM),
            preferred_element_type=jnp.float32,
        )
        * score_scale
    )
    allowed = video_clip[:, None, None] == query_clip[None, None, :]
    scores = jnp.where(allowed, scores, masked_floor)
    row_max = jnp.max(scores, axis=2, keepdims=True)
    weights = jnp.where(allowed, jnp.exp(scores - row_max), 0.0)
    video_totals = jnp.sum(weights, axis=2)
    video_mixed = jnp.einsum(
        "qhk,khd->qhd",
        weights.astype(jnp.bfloat16),
        every_value.reshape(audio_total, local_heads, HEAD_DIM),
        preferred_element_type=jnp.float32,
    )
    video_attn = (
        (video_mixed / video_totals[:, :, None])
        .reshape(video_rows, local_width)
        .astype(jnp.bfloat16)
    )
    video_proj = jnp.dot(
        lax.all_gather(video_attn, "head", axis=1, tiled=True),
        video_out_weight,
        preferred_element_type=jnp.float32,
    )
    query_block = math.gcd(audio_total, 512)
    block_count = audio_total // query_block
    video_key_heads = video_k.reshape(video_rows, local_heads, HEAD_DIM)
    video_value_heads = video_v.reshape(video_rows, local_heads, HEAD_DIM)

    def partial_block(paired):
        query_part, clip_part = paired
        block_scores = (
            jnp.einsum(
                "qhd,khd->qhk",
                query_part.reshape(query_block, local_heads, HEAD_DIM),
                video_key_heads,
                preferred_element_type=jnp.float32,
            )
            * score_scale
        )
        permitted = clip_part[:, None, None] == video_clip[None, None, :]
        block_scores = jnp.where(permitted, block_scores, masked_floor)
        local_max = jnp.max(block_scores, axis=2)
        block_weights = jnp.where(permitted, jnp.exp(block_scores - local_max[:, :, None]), 0.0)
        totals = jnp.sum(block_weights, axis=2)
        weighted = jnp.einsum(
            "qhk,khd->qhd",
            block_weights.astype(jnp.bfloat16),
            video_value_heads,
            preferred_element_type=jnp.float32,
        ).reshape(query_block, local_width)
        return (local_max, totals, weighted)

    local_max, totals, weighted = lax.map(
        partial_block,
        (
            every_query.reshape(block_count, query_block, local_width),
            query_clip.reshape(block_count, query_block),
        ),
    )
    local_max = local_max.reshape(audio_total, local_heads)
    totals = totals.reshape(audio_total, local_heads)
    weighted = weighted.reshape(audio_total, local_width)
    global_max = taken_together(local_max, SEQ)
    factor = jnp.exp(local_max - global_max)
    scaled_sum = (
        weighted.reshape(audio_total, local_heads, HEAD_DIM) * factor[:, :, None]
    ).reshape(audio_total, local_width)
    own_sum, own_total = sent_together_2(
        (scaled_sum, totals * factor), (("seq_0", "seq_1"), "seq_2"), 0, 1
    )
    audio_attn = (
        (own_sum.reshape(audio_rows, local_heads, HEAD_DIM) / own_total[:, :, None])
        .reshape(audio_rows, local_width)
        .astype(jnp.bfloat16)
    )
    audio_full = gathered_copies(audio_attn, "head", 1)
    audio_proj = jnp.dot(audio_full, audio_out_weight, preferred_element_type=jnp.float32)
    return (video_proj.astype(jnp.bfloat16), audio_proj.astype(jnp.bfloat16))


def solution(mesh):
    finer = Mesh(
        mesh.devices.reshape(8, 4, 2, mesh.shape["head"]), ("seq_0", "seq_1", "seq_2", "head")
    )
    placed = (
        P(SEQ, "head"),
        P(SEQ, "head"),
        P(SEQ, "head"),
        P(SEQ, "head"),
        P(SEQ, "head"),
        P(SEQ, "head"),
        P(),
        P(),
        P(None, "head"),
        P(None, "head"),
    )
    return jax.shard_map(
        per_device,
        mesh=finer,
        in_specs=placed,
        out_specs=(P(SEQ, "head"), P(SEQ, "head")),
        check_vma=False,
    )
```

profile of v0, /device:TPU:2, one launch (start us, length us, event | category | flops | bytes accessed | tf_op | source)
XLA Modules:
  0.0 135.7 jit_solution(13302887809576837175)
XLA Ops:
  0.6 0.0 copy-start
  0.7 0.9 pad_maximum_fusion
  1.6 0.9 broadcast_in_dim.91
  2.5 11.6 %all-to-all-start = ((bf16[32,8,1536]{2,1,0:T(8,128)(2,1)}), bf16[32,8,1536]{2,1,0:T(8,128)(2,1)S(1)}, u32[]{:S(2)}, u32[]{:S(2)}) async-start(bf16[32,8,1536]{2,1,0:T(8,128)(2,1)} %broadcast_in_dim.91), calls=%async_computation | async-start | bytes 1572864 | tf_op jit(solution)/shard_map/all_to_all | solution.py:18
  14.1 0.2 reduce-window.16
  14.3 0.2 reduce-window.17
  14.5 0.1 copy.48
  14.6 0.1 convert_reduce_fusion.1
  14.7 0.1 convert_reduce_fusion
  14.8 0.1 broadcast_compare_fusion
  15.0 21.6 %all-to-all-done = bf16[32,8,1536]{2,1,0:T(8,128)(2,1)S(1)} async-done(((bf16[32,8,1536]{2,1,0:T(8,128)(2,1)}), bf16[32,8,1536]{2,1,0:T(8,128)(2,1)S(1)}, u32[]{:S(2)}, u32[]{:S(2)}) %all-to-all-start) | async-done | bytes 786464 | tf_op jit(solution)/shard_map/all_to_all | solution.py:18
  36.6 0.1 broadcast_in_dim.92
  36.7 5.0 %all_to_all.30 = bf16[2,32,8,1536]{3,2,1,0:T(8,128)(2,1)S(1)} all-to-all(bf16[2,32,8,1536]{3,2,1,0:T(8,128)(2,1)S(1)} %broadcast_in_dim.92), channel_id=1, replica_groups=mesh['seq_0'=8,'seq_1'=4,'seq_2'=2,'head'=4] {'seq_2'}, dimensions={0} | all-to-all | bytes 3145728 | tf_op jit(solution)/shard_map/all_to_all | solution.py:18
  41.7 0.2 copy.42
  41.9 1.1 fusion.36
  43.0 0.2 copy.47
  43.2 1.9 %bitcast_reduce_fusion = (f32[512,8]{0,1:T(8,128)S(1)}, f32[8,512,128]{2,1,0:T(8,128)}) fusion(pred[512,128]{1,0:T(8,128)(4,1)S(1)} %broadcast_compare_fusion, bf16[512,8,64]{0,2,1:T(8,128)(2,1)S(1)} %bitcast.66, bf16[128,8,64]{0,2,1:T(8,128)(2,1)S(1)} %bitcast.70), kind=kOutput, calls=%fused_computation.2 | convolution fusion | flops 68677632 | bytes 2834432 | tf_op jit(solution)/shard_map/while/body/eval_jaxpr/qhd,khd->qhk/dot_general | solution.py:156
  45.1 1.1 broadcast_in_dim.100
  46.2 6.0 %all-to-all-start.2 = ((f32[64,512,8]{1,2,0:T(8,128)}), f32[64,512,8]{1,2,0:T(8,128)S(1)}, u32[]{:S(2)}, u32[]{:S(2)}) async-start(f32[64,512,8]{1,2,0:T(8,128)} %broadcast_in_dim.100), calls=%async_computation.2 | async-start | bytes 2097152 | tf_op jit(solution)/shard_map/all_to_all | solution.py:18
  52.2 0.8 copy.50
  52.9 2.5 %fusion.4 = f32[512,8]{0,1:T(8,128)S(1)} fusion(f32[8,512,128]{2,1,0:T(8,128)} %get-tuple-element.26, f32[512,8]{0,1:T(8,128)S(1)} %get-tuple-element.25, pred[512,128]{1,0:T(8,128)(4,1)S(1)} %broadcast_compare_fusion), kind=kLoop, calls=%fused_computation.9 | loop fusion | flops 2617344 | bytes 2195456 | tf_op jit(solution)/shard_map/while/body/eval_jaxpr/reduce_sum | solution.py:168
  55.5 25.5 %all-to-all-done.2 = f32[64,512,8]{1,2,0:T(8,128)S(1)} async-done(((f32[64,512,8]{1,2,0:T(8,128)}), f32[64,512,8]{1,2,0:T(8,128)S(1)}, u32[]{:S(2)}, u32[]{:S(2)}) %all-to-all-start.2) | async-done | bytes 1048608 | tf_op jit(solution)/shard_map/all_to_all | solution.py:18
  81.0 0.1 reduce_max.30
  81.1 0.1 copy.56
  81.2 2.3 %fusion.6 = f32[512,8,64]{0,2,1:T(8,128)S(1)} fusion(bf16[128,8,64]{0,2,1:T(8,128)(2,1)} %bitcast.76, f32[8,512,128]{2,1,0:T(8,128)} %get-tuple-element.26, f32[512,8]{0,1:T(8,128)S(1)} %get-tuple-element.25, pred[512,128]{1,0:T(8,128)(4,1)S(1)} %broadcast_compare_fusion, f32[512,8]{0,1:T(8,128)S(1)} %get-tuple-element.21), kind=kOutput, calls=%fused_computation.12 | convolution fusion | flops 69992448 | bytes 3375104 | tf_op jit(solution)/shard_map/while/body/eval_jaxpr/qhk,khd->qhd/dot_general | solution.py:169
  83.5 2.0 %copy.51 = f32[512,8,64]{2,1,0:T(8,128)} copy(f32[512,8,64]{0,2,1:T(8,128)S(1)} %fusion.6) | data formatting | bytes 2097152 | tf_op jit(solution)/shard_map/mul | solution.py:190
  85.5 1.9 %mul.52 = f32[32,2,8,512]{3,2,1,0:T(8,128)S(1)} reshape(f32[512,8,64]{2,1,0:T(8,128)} %copy.51) | data formatting | bytes 2097152 | tf_op jit(solution)/shard_map/mul | solution.py:190
  87.4 0.1 maximum_bitcast_fusion
  87.5 0.1 copy.53
  87.6 4.8 %all_to_all.31 = f32[2,32,8,520]{3,2,1,0:T(8,128)S(1)} all-to-all(f32[2,32,8,520]{3,2,1,0:T(8,128)S(1)} %copy.53), channel_id=1, replica_groups=mesh['seq_0'=8,'seq_1'=4,'seq_2'=2,'head'=4] {'seq_2'}, dimensions={0} | all-to-all | bytes 2129920 | tf_op jit(solution)/shard_map/all_to_all | solution.py:57
  92.4 1.0 reduce_sum.59
  93.4 5.4 %all-to-all-start.4 = ((f32[32,8,520]{2,1,0:T(8,128)}), f32[32,8,520]{2,1,0:T(8,128)S(1)}, u32[]{:S(2)}, u32[]{:S(2)}) async-start(f32[32,8,520]{2,1,0:T(8,128)} %reduce_sum.59), calls=%async_computation.4 | async-start | bytes 1310720 | tf_op jit(solution)/shard_map/all_to_all | solution.py:64
  98.8 0.8 broadcast_compare_fusion.1
  99.6 0.1 copy.45
  99.7 2.1 %copy.43 = bf16[512,512]{0,1:T(8,128)(2,1)} copy(bf16[512,512]{1,0:T(8,128)(2,1)} %get-tuple-element.24) | data formatting | bytes 1048576 | tf_op jit(solution)/shard_map/slice | solution.py:40
  101.8 1.0 copy.44
  102.8 2.1 %fusion.37 = f32[128,8]{0,1:T(8,128)S(1)} fusion(pred[128,512]{0,1:T(8,128)(4,1)S(1)} %copy-done.6, bf16[512,8,64]{0,2,1:T(8,128)(2,1)} %bitcast.67, bf16[128,8,64]{0,2,1:T(8,128)(2,1)S(1)} %bitcast.72), kind=kOutput, calls=%fused_computation.54 | convolution fusion | flops 69730816 | bytes 724992 | tf_op jit(solution)/shard_map/sub | solution.py:130
  104.9 1.8 %fusion.38 = f32[8,512,128]{2,1,0:T(8,128)} fusion(bf16[512,8,64]{0,2,1:T(8,128)(2,1)S(1)} %bitcast.68, bf16[128,8,64]{0,2,1:T(8,128)(2,1)S(1)} %bitcast.73), kind=kOutput, calls=%fused_computation.55 | convolution fusion | flops 67108864 | bytes 2752512 | tf_op jit(solution)/shard_map/qhd,khd->qhk/dot_general | solution.py:119
  106.8 3.9 %fusion.8 = bf16[128,8,64]{0,2,1:T(8,128)(2,1)S(1)} fusion(bf16[512,8,64]{0,2,1:T(8,128)(2,1)} %bitcast.71, f32[8,512,128]{2,1,0:T(8,128)} %fusion.38, pred[128,512]{0,1:T(8,128)(4,1)S(1)} %copy-done.6, f32[128,8]{0,1:T(8,128)S(1)} %fusion.37), kind=kOutput, calls=%fused_computation.17 | convolution fusion | flops 69862912 | bytes 2822144 | tf_op jit(solution)/shard_map/qhk,khd->qhd/dot_general | solution.py:132
  110.6 13.3 %all_gather.3 = bf16[128,2048]{0,1:T(8,128)(2,1)S(1)} all-gather(bf16[128,512]{0,1:T(8,128)(2,1)S(1)} %bitcast.75), channel_id=1, replica_groups=mesh['seq_0'=8,'seq_1'=4,'seq_2'=2,'head'=4] {'head'}, dimensions={1}, use_global_device_ids=true | all-gather | bytes 655360 | tf_op jit(solution)/shard_map/all_gather | solution.py:144
  123.9 0.1 reduce_sum.60
  124.0 0.1 div.21
  124.1 0.1 div.22
  124.2 0.6 broadcast_in_dim.101
  124.8 4.4 %all-to-all-start.5 = ((bf16[4,8,512]{2,1,0:T(8,128)(2,1)}), bf16[4,8,512]{2,1,0:T(8,128)(2,1)S(1)}, u32[]{:S(2)}, u32[]{:S(2)}) async-start(bf16[4,8,512]{2,1,0:T(8,128)(2,1)} %broadcast_in_dim.101), calls=%async_computation.5 | async-start | bytes 65536 | tf_op jit(solution)/shard_map/all_to_all | solution.py:18
  129.2 3.6 %convolution_convert_fusion = bf16[128,1024]{1,0:T(8,128)(2,1)} fusion(bf16[128,2048]{0,1:T(8,128)(2,1)S(1)} %all_gather.3, bf16[2048,1024]{1,0:T(8,128)(2,1)} %param.18), kind=kOutput, calls=%fused_computation.14 | convolution fusion | flops 537001984 | bytes 4980736 | tf_op jit(solution)/shard_map/dot_general | solution.py:143
  132.9 1.8 %all-to-all-done.5 = bf16[4,8,512]{2,1,0:T(8,128)(2,1)S(1)} async-done(((bf16[4,8,512]{2,1,0:T(8,128)(2,1)}), bf16[4,8,512]{2,1,0:T(8,128)(2,1)S(1)}, u32[]{:S(2)}, u32[]{:S(2)}) %all-to-all-start.5) | async-done | bytes 32800 | tf_op jit(solution)/shard_map/all_to_all | solution.py:18
  134.7 1.0 convolution_convert_fusion.1
  (23 shorter events, 0.1 us)
Async XLA Ops:
  0.6 134.0 %copy-start = (bf16[2048,512]{1,0:T(8,128)(2,1)S(1)}, bf16[2048,512]{1,0:T(8,128)(2,1)}, u32[]{:S(2)}) copy-start(bf16[2048,512]{1,0:T(8,128)(2,1)} %param.19) | copy-start | bytes 6291460
  0.6 13.5 %copy-start.7 = (s32[4]{0:T(128)S(1)}, s32[4]{0:T(128)}, u32[]{:S(2)}) copy-start(s32[4]{0:T(128)} %param.16) | copy-start | bytes 52
  0.7 13.7 %copy-start.8 = (s32[4]{0:T(128)S(1)}, s32[4]{0:T(128)}, u32[]{:S(2)}) copy-start(s32[4]{0:T(128)} %param.17) | copy-start | bytes 52
  0.7 13.8 %copy-start.3 = (bf16[128,512]{1,0:T(8,128)(2,1)S(1)}, bf16[128,512]{1,0:T(8,128)(2,1)}, u32[]{:S(2)}) copy-start(bf16[128,512]{1,0:T(8,128)(2,1)} %param.11) | copy-start | bytes 393220
  2.5 34.1 %all-to-all-start = ((bf16[32,8,1536]{2,1,0:T(8,128)(2,1)}), bf16[32,8,1536]{2,1,0:T(8,128)(2,1)S(1)}, u32[]{:S(2)}, u32[]{:S(2)}) async-start(bf16[32,8,1536]{2,1,0:T(8,128)(2,1)} %broadcast_in_dim.91), calls=%async_computation | async-start | bytes 1572864 | tf_op jit(solution)/shard_map/all_to_all | solution.py:18
  45.1 7.1 %copy-start.4 = (bf16[128,512]{1,0:T(8,128)(2,1)S(1)}, bf16[128,512]{1,0:T(8,128)(2,1)}, u32[]{:S(2)}) copy-start(bf16[128,512]{1,0:T(8,128)(2,1)} %param.12) | copy-start | bytes 393220
  46.2 34.8 %all-to-all-start.2 = ((f32[64,512,8]{1,2,0:T(8,128)}), f32[64,512,8]{1,2,0:T(8,128)S(1)}, u32[]{:S(2)}, u32[]{:S(2)}) async-start(f32[64,512,8]{1,2,0:T(8,128)} %broadcast_in_dim.100), calls=%async_computation.2 | async-start | bytes 2097152 | tf_op jit(solution)/shard_map/all_to_all | solution.py:18
  92.4 7.2 %copy-start.5 = (bf16[128,512]{1,0:T(8,128)(2,1)S(1)}, bf16[128,512]{1,0:T(8,128)(2,1)}, u32[]{:S(2)}) copy-start(bf16[128,512]{1,0:T(8,128)(2,1)} %param.10) | copy-start | bytes 393220
  93.4 8.4 %copy-start.1 = (bf16[512,512]{1,0:T(8,128)(2,1)S(1)}, bf16[512,512]{1,0:T(8,128)(2,1)}, u32[]{:S(2)}) copy-start(bf16[512,512]{1,0:T(8,128)(2,1)} %get-tuple-element.23) | copy-start | bytes 1572868
  93.4 30.5 %all-to-all-start.4 = ((f32[32,8,520]{2,1,0:T(8,128)}), f32[32,8,520]{2,1,0:T(8,128)S(1)}, u32[]{:S(2)}, u32[]{:S(2)}) async-start(f32[32,8,520]{2,1,0:T(8,128)} %reduce_sum.59), calls=%async_computation.4 | async-start | bytes 1310720 | tf_op jit(solution)/shard_map/all_to_all | solution.py:64
  99.7 3.1 %copy-start.6 = (pred[128,512]{0,1:T(8,128)(4,1)S(1)}, pred[128,512]{0,1:T(8,128)(4,1)}, u32[]{:S(2)}) copy-start(pred[128,512]{0,1:T(8,128)(4,1)} %broadcast_compare_fusion.1) | copy-start | bytes 196612
  102.8 2.1 %copy-start.2 = (bf16[512,512]{0,1:T(8,128)(2,1)S(1)}, bf16[512,512]{0,1:T(8,128)(2,1)}, u32[]{:S(2)}) copy-start(bf16[512,512]{0,1:T(8,128)(2,1)} %copy.44) | copy-start | bytes 1572868
  124.8 9.9 %all-to-all-start.5 = ((bf16[4,8,512]{2,1,0:T(8,128)(2,1)}), bf16[4,8,512]{2,1,0:T(8,128)(2,1)S(1)}, u32[]{:S(2)}, u32[]{:S(2)}) async-start(bf16[4,8,512]{2,1,0:T(8,128)(2,1)} %broadcast_in_dim.101), calls=%async_computation.5 | async-start | bytes 65536 | tf_op jit(solution)/shard_map/all_to_all | solution.py:18
where the time goes:
time: 136 us
  waiting for transfers between devices  48.9 us (36%)
  starting transfers between devices  27.4 us (20%)
  blocking collectives  23.1 us (17%)
  matrix products  16.6 us (12%)
  local copies, waits for them, and re-layouts  12.7 us (9%)
  other arithmetic  6.14 us (5%)
    all_to_all x3, waiting for transfers between devices, sent_to_all(): lax.all_to_all(jnp.broadcast_to(value[None], (count, *value.shape)), axis...  48.9 us
    all_to_all x3, starting transfers between devices, sent_to_all(): lax.all_to_all(jnp.broadcast_to(value[None], (count, *value.shape)), axis...  22 us
    all_gather x1, blocking collectives, per_device(): lax.all_gather(video_attn, 'head', axis=1, tiled=True)  13.3 us
    all_to_all x1, starting transfers between devices, sum_by_axis(): return jnp.sum(lax.all_to_all(own, far, 0, 0, tiled=True), axis=0)  5.38 us
    all_to_all x1, blocking collectives, sent_to_all(): lax.all_to_all(jnp.broadcast_to(value[None], (count, *value.shape)), axis...  5 us
    all_to_all x1, blocking collectives, sum_at_owner(): lax.all_to_all(in_blocks(value, dim, count), axis, 0, 0, tiled=True)  4.79 us
    slice x4, local copies, waits for them, and re-layouts, sent_together(): lax.slice_in_dim(filled, at, at + a.shape[along], axis=along)  4.41 us
    mul x2, local copies, waits for them, and re-layouts, per_device(): weighted.reshape(audio_total, local_heads, HEAD_DIM) * factor[:, :, None]  3.92 us
  transfers between devices with their start and end apart: 4, of which 3 were waited for; matrix products, arithmetic and copies ran while one was open for 14% of the time, Pallas kernels for 0%

commit v1 on v0

v1 whole, which is shorter than its diff:
```python
import math

import jax
import jax.numpy as jnp
from jax import lax
from jax.experimental import pallas as pl
from jax.experimental.pallas import tpu as pltpu
from jax.sharding import PartitionSpec as P

HEAD_DIM = 64
GROUP = 8
MESH = pl.DeviceIdType.MESH
BF = jnp.bfloat16
F32 = jnp.float32
FORBID = -65536.0
LOG2E = math.log2(math.e)
SCALE = LOG2E / math.sqrt(HEAD_DIM)


def nt_dot(a, b):
    return lax.dot_general(a, b, (((1,), (1,)), ((), ())), preferred_element_type=F32)


def nn_dot(a, b):
    return lax.dot_general(a, b, (((1,), (0,)), ((), ())), preferred_element_type=F32)


def swap(x):
    return pltpu.roll(x, 64, x.ndim - 1)


def kernel(
    nz, ny,
    vl, al, vq, vk, vv, aq, ak, av, wv_hbm, wa_hbm,
    vo, ao,
    inq, ink, inv, ina_q, ina_k, ina_v, wv, wa,
    tok_aug, aud_aug,
    sendq, sendkv, senda, recvq, recvkv, recva,
    zkv, zq, kk, v0, v1,
    sendo, recvo, sendr, recvr, sendf, recvf, attn, aud,
    in_sem,
    q_s, q_r, kv_s, kv_r, a_s, a_r, zk_s, zk_r, zq_s, zq_r, r_s, r_r, o_s, o_r, f_s, f_r,
):
    s = lax.axis_index("seq")
    y = lax.axis_index("head")
    z = s // GROUP
    j = lax.rem(s, GROUP)
    at = nz * 64

    def loop(lo, hi, body):
        def step(i, carry):
            body(i)
            return carry
        lax.fori_loop(lo, hi, step, 0)

    def in_group(d):
        return lax.rem(j + d, GROUP)

    def in_ring(d):
        return lax.rem(z + d, nz)

    def peer(zz, jj, yy):
        return (zz * GROUP + jj, yy)

    def remote(src, dst, ss, rs, to):
        return pltpu.make_async_remote_copy(
            src_ref=src, dst_ref=dst, send_sem=ss, recv_sem=rs, device_id=to, device_id_type=MESH
        )

    local = [
        pltpu.make_async_copy(src, dst, in_sem.at[i])
        for i, (src, dst) in enumerate(
            [(aq, ina_q), (ak, ina_k), (av, ina_v), (vq, inq), (vk, ink), (vv, inv), (wv_hbm, wv), (wa_hbm, wa)]
        )
    ]
    for c in local:
        c.start()

    barrier = pltpu.get_barrier_semaphore()

    def greet_out(i):
        n = i + 1
        pl.semaphore_signal(
            barrier, inc=1,
            device_id=peer(z, lax.rem(j + lax.rem(n, GROUP), GROUP), lax.rem(y + n // GROUP, ny)),
            device_id_type=MESH,
        )

    loop(0, GROUP * ny - 1, greet_out)

    def greet_ring(d):
        pl.semaphore_signal(barrier, inc=1, device_id=peer(in_ring(d), j, y), device_id_type=MESH)

    loop(1, nz, greet_ring)

    v_end = [vl[0]]
    a_end = [al[0]]
    for c in range(1, 4):
        v_end.append(v_end[-1] + vl[c])
        a_end.append(a_end[-1] + al[c])

    def clip_of(pos, ends):
        total = jnp.zeros_like(pos)
        for e in ends:
            total = total + (pos >= e).astype(jnp.int32)
        return total

    blk = lax.broadcasted_iota(jnp.int32, (GROUP, 64, 128), 0)
    row = lax.broadcasted_iota(jnp.int32, (GROUP, 64, 128), 1)
    lane = lax.broadcasted_iota(jnp.int32, (GROUP, 64, 128), 2)
    token = (z * GROUP + blk) * 128 + row + jnp.where(lane < 4, 0, 64)
    mark = jnp.where(lane < 4, lane, lane - 4)
    one_hot = (lane < 8) & (clip_of(token, v_end) == mark)
    tok_aug[...] = jnp.where(one_hot, 1.0, 0.0).astype(BF)

    blk = lax.broadcasted_iota(jnp.int32, (nz, 64, 128), 0)
    row = lax.broadcasted_iota(jnp.int32, (nz, 64, 128), 1)
    lane = lax.broadcasted_iota(jnp.int32, (nz, 64, 128), 2)
    pos = blk * 64 + row + at // 2
    pos = jnp.where(pos >= at, pos - at, pos)
    a_clip = clip_of(pos, a_end)
    aud_aug[0] = jnp.where((lane < 4) & (a_clip != lane), FORBID, 0.0).astype(BF)
    aud_aug[1] = jnp.where((lane >= 4) & (lane < 8) & (a_clip != lane - 4), FORBID, 0.0).astype(BF)

    def low(shape):
        return lax.broadcasted_iota(jnp.int32, shape, len(shape) - 1) < 64

    for i in range(3):
        local[i].wait()
    low8 = low((8, 128))
    for p in range(4):
        cols = pl.ds(128 * p, 128)
        q8, k8, v8 = (r[:, cols].astype(F32) for r in (ina_q, ina_k, ina_v))
        even = jnp.concatenate([jnp.where(low8, k8, swap(v8)), q8], axis=0)
        odd = jnp.concatenate([jnp.where(low8, swap(k8), v8), swap(q8)], axis=0)
        senda[2 * p] = even.astype(BF)
        senda[2 * p + 1] = odd.astype(BF)

    low64 = low((64, 128))

    def halves(ref, put):
        for p in range(4):
            cols = pl.ds(128 * p, 128)
            top = ref[0:64, cols].astype(F32)
            bottom = ref[64:128, cols].astype(F32)
            put(2 * p, jnp.where(low64, top, swap(bottom)).astype(BF))
            put(2 * p + 1, jnp.where(low64, swap(top), bottom).astype(BF))

    def put_q(h, x):
        sendq[h] = x

    def put_k(h, x):
        sendkv[h, 0] = x

    def put_v(h, x):
        sendkv[h, 1] = x

    local[3].wait()
    halves(inq, put_q)

    pl.semaphore_wait(barrier, GROUP * ny - 1 + nz - 1)

    def a_copy(t):
        return remote(senda.at[t], recva.at[j], a_s.at[t], a_r.at[j], peer(z, t, y))

    def q_copy(t):
        return remote(sendq.at[t], recvq.at[j], q_s.at[t], q_r.at[j], peer(z, t, y))

    def kv_copy(t):
        return remote(sendkv.at[t], recvkv.at[j], kv_s.at[t], kv_r.at[j], peer(z, t, y))

    def arrived(dst, rs):
        remote(dst, dst, rs, rs, peer(z, in_group(1), y)).wait_recv()

    loop(1, GROUP, lambda d: a_copy(in_group(d)).start())
    loop(1, GROUP, lambda d: q_copy(in_group(d)).start())
    local[4].wait()
    halves(ink, put_k)
    local[5].wait()
    halves(inv, put_v)
    loop(1, GROUP, lambda d: kv_copy(in_group(d)).start())
    recva[j] = senda[j]
    recvq[j] = sendq[j]
    recvkv[j] = sendkv[j]

    def wait_a(d):
        t = in_group(d)
        arrived(recva.at[t], a_r.at[t])

    loop(1, GROUP, wait_a)
    got = recva[...].astype(F32)
    zkv[z] = got[:, 0:8, :].reshape(64, 128).astype(BF)
    q64 = got[:, 8:16, :].reshape(64, 128)
    zq[z] = jnp.where(low((32, 128)), q64[0:32], swap(q64[32:64])).astype(BF)

    def zk_copy(d):
        t = in_ring(d)
        return remote(zkv.at[z], zkv.at[z], zk_s.at[t], zk_r.at[z], peer(t, j, y))

    def zq_copy(d):
        t = in_ring(d)
        return remote(zq.at[z], zq.at[z], zq_s.at[t], zq_r.at[z], peer(t, j, y))

    loop(1, nz, lambda d: zk_copy(d).start())
    loop(1, nz, lambda d: zq_copy(d).start())

    def wait_zk(d):
        t = in_ring(d)
        arrived(zkv.at[t], zk_r.at[t])

    loop(1, nz, wait_zk)
    kv = zkv[...].reshape(at, 128).astype(F32)
    vk_ = swap(kv)
    low_at = low((at, 128))
    kk[0:at] = jnp.where(low_at, kv, 0.0).astype(BF)
    kk[at : 2 * at] = jnp.where(low_at, 0.0, vk_).astype(BF)
    v0[...] = jnp.where(low_at, vk_, 1.0).astype(BF)
    v1[...] = jnp.where(low_at, 1.0, kv).astype(BF)

    def wait_q(d):
        t = in_group(d)
        arrived(recvq.at[t], q_r.at[t])

    loop(1, GROUP, wait_q)

    def o_copy(t, e):
        u = lax.rem(y + e, ny)
        return remote(sendo.at[t], recvo.at[y, j], o_s.at[u, t], o_r.at[y, j], peer(z, t, u))

    def video_block(t):
        query = jnp.concatenate([recvq[t], tok_aug[t]], axis=1)
        keys = jnp.concatenate([kk[0 : 2 * at], aud_aug[...].reshape(2 * at, 128)], axis=1)
        sc = nt_dot(query, keys)
        outs = []
        for half, values in ((sc[:, 0:at], v0), (sc[:, at : 2 * at], v1)):
            top = jnp.max(half, axis=1, keepdims=True)
            w = jnp.exp2((half - top) * SCALE).astype(BF)
            outs.append(nn_dot(w, values[...]))
        num = jnp.where(low64, outs[0], outs[1])
        den = swap(jnp.where(low64, outs[1], outs[0]))
        return (num / den).astype(BF)

    def video_step(d):
        t = in_group(d)
        sendo[t] = video_block(t)
        loop(0, ny, lambda e: o_copy(t, e).start())

    loop(1, GROUP, video_step)
    sendo[j] = video_block(j)
    loop(1, ny, lambda e: o_copy(j, e).start())
    recvo[y, j] = sendo[j]

    def wait_kv(d):
        t = in_group(d)
        arrived(recvkv.at[t], kv_r.at[t])

    loop(1, GROUP, wait_kv)

    def wait_zq(d):
        t = in_ring(d)
        arrived(zq.at[t], zq_r.at[t])

    loop(1, nz, wait_zq)
    low_gt = low((GROUP * 64, 128))
    vp = recvkv[:, 1].reshape(GROUP * 64, 128).astype(F32)
    v0g = jnp.where(low_gt, vp, 1.0).astype(BF)
    v1g = jnp.where(low_gt, 1.0, vp).astype(BF)
    kk[0 : GROUP * 64] = v0g
    kk[GROUP * 64 : 2 * GROUP * 64] = v1g
    low32 = low((32, 128))
    lane64 = lax.broadcasted_iota(jnp.int32, (64, 128), 1)

    def audio_block(t):
        qp = zq[t].astype(F32)
        qs = swap(qp)
        query = jnp.concatenate(
            [
                jnp.where(low32, qp, 0.0), jnp.where(low32, qs, 0.0),
                jnp.where(low32, 0.0, qs), jnp.where(low32, 0.0, qp),
            ],
            axis=0,
        ).astype(BF)
        query = jnp.concatenate([query, aud_aug[:, t].reshape(128, 128)], axis=1)
        keys = jnp.concatenate(
            [recvkv[:, 0].reshape(GROUP * 64, 128), tok_aug[...].reshape(GROUP * 64, 128)], axis=1
        )
        sc = nt_dot(query, keys)
        top = jnp.max(sc, axis=1, keepdims=True)
        top = jnp.maximum(top[0:64], top[64:128])
        w0 = jnp.exp2((sc[0:64] - top) * SCALE).astype(BF)
        w1 = jnp.exp2((sc[64:128] - top) * SCALE).astype(BF)
        full = nn_dot(w0, kk[0 : GROUP * 64]) + swap(nn_dot(w1, kk[GROUP * 64 : 2 * GROUP * 64]))
        mean = full / swap(full)
        level = top * SCALE + jnp.log(jnp.where(low64, 1.0, full)) * LOG2E
        first = level.astype(BF).astype(F32)
        second = (level - first).astype(BF).astype(F32)
        third = level - first - second
        parts = jnp.where(lane64 < 96, first, jnp.where(lane64 < 112, second, third))
        return jnp.where(low64, mean, parts).astype(BF)

    def r_copy(d):
        t = in_ring(d)
        return remote(sendr.at[t], recvr.at[z], r_s.at[t], r_r.at[z], peer(t, j, y))

    def audio_step(d):
        t = in_ring(d)
        sendr[t] = audio_block(t)
        r_copy(d).start()

    loop(1, nz, audio_step)
    recvr[z] = audio_block(z)

    def wait_r(d):
        t = in_ring(d)
        arrived(recvr.at[t], r_r.at[t])

    loop(1, nz, wait_r)
    part = recvr[...].astype(F32)
    level = part[:, :, 64:65] + part[:, :, 96:97] + part[:, :, 112:113]
    share = jnp.exp2(level - jnp.max(level, axis=0, keepdims=True))
    mixed = jnp.sum(part * share, axis=0) / jnp.sum(share, axis=0)
    sendf[...] = mixed.reshape(GROUP, 8, 128)

    def f_copy(n):
        t = lax.rem(j + lax.rem(n, GROUP), GROUP)
        u = lax.rem(y + n // GROUP, ny)
        return remote(sendf.at[t], recvf.at[y, j], f_s.at[u, t], f_r.at[y, j], peer(z, t, u))

    loop(1, GROUP * ny, lambda n: f_copy(n).start())
    recvf[y, j] = sendf[j]

    def wait_o(n):
        t = lax.rem(j + lax.rem(n, GROUP), GROUP)
        u = lax.rem(y + n // GROUP, ny)
        arrived(recvo.at[u, t], o_r.at[u, t])

    loop(1, GROUP * ny, wait_o)
    for u in range(ny):
        for x in range(GROUP // 2):
            cols = pl.ds((u * 4 + x) * 128, 128)
            a0 = recvo[u, 2 * x].astype(F32)
            a1 = recvo[u, 2 * x + 1].astype(F32)
            attn[0:64, cols] = jnp.where(low64, a0, swap(a1)).astype(BF)
            attn[64:128, cols] = jnp.where(low64, swap(a0), a1).astype(BF)
    local[6].wait()
    width = wv.shape[1] // 4
    for n in range(4):
        cols = pl.ds(n * width, width)
        vo[:, cols] = nn_dot(attn[...], wv[:, cols]).astype(BF)

    def wait_f(n):
        t = lax.rem(j + lax.rem(n, GROUP), GROUP)
        u = lax.rem(y + n // GROUP, ny)
        arrived(recvf.at[u, t], f_r.at[u, t])

    loop(1, GROUP * ny, wait_f)
    for u in range(ny):
        for x in range(GROUP // 2):
            cols = pl.ds((u * 4 + x) * 128, 128)
            aud[:, cols] = jnp.where(low8, recvf[u, 2 * x], swap(recvf[u, 2 * x + 1]))
    local[7].wait()
    ao[...] = nn_dot(aud[...].astype(BF), wa[...]).astype(BF)

    def sent_group(d):
        t = in_group(d)
        a_copy(t).wait_send()
        q_copy(t).wait_send()
        kv_copy(t).wait_send()

    def sent_ring(d):
        zk_copy(d).wait_send()
        zq_copy(d).wait_send()
        r_copy(d).wait_send()

    def sent_out(n):
        t = lax.rem(j + lax.rem(n, GROUP), GROUP)
        o_copy(t, n // GROUP).wait_send()
        f_copy(n).wait_send()

    loop(1, GROUP, sent_group)
    loop(1, nz, sent_ring)
    loop(1, GROUP * ny, sent_out)


def per_device(nz, ny, vq, vk, vv, aq, ak, av, vl, al, wv, wa):
    rows, width = vq.shape
    a_rows = aq.shape[0]
    at = nz * 64
    hbm = pl.BlockSpec(memory_space=pl.ANY)
    smem = pl.BlockSpec(memory_space=pltpu.SMEM)
    vmem = pl.BlockSpec(memory_space=pltpu.VMEM)
    bf = lambda *shape: pltpu.VMEM(shape, BF)
    dma = lambda *shape: pltpu.SemaphoreType.DMA(shape)

    def body(*refs):
        kernel(nz, ny, *refs)

    return pl.pallas_call(
        body,
        out_shape=(
            jax.ShapeDtypeStruct((rows, wv.shape[1]), BF),
            jax.ShapeDtypeStruct((a_rows, wa.shape[1]), BF),
        ),
        in_specs=[smem, smem] + [hbm] * 8,
        out_specs=(vmem, vmem),
        scratch_shapes=[
            bf(rows, width), bf(rows, width), bf(rows, width),
            bf(a_rows, width), bf(a_rows, width), bf(a_rows, width),
            bf(*wv.shape), bf(*wa.shape),
            bf(GROUP, 64, 128), bf(2, nz, 64, 128),
            bf(GROUP, 64, 128), bf(GROUP, 2, 64, 128), bf(GROUP, 16, 128),
            bf(GROUP, 64, 128), bf(GROUP, 2, 64, 128), bf(GROUP, 16, 128),
            bf(nz, 64, 128), bf(nz, 32, 128),
            bf(2 * max(at, GROUP * 64), 128), bf(at, 128), bf(at, 128),
            bf(GROUP, 64, 128), bf(ny, GROUP, 64, 128),
            bf(nz, 64, 128), bf(nz, 64, 128),
            pltpu.VMEM((GROUP, 8, 128), F32), pltpu.VMEM((ny, GROUP, 8, 128), F32),
            bf(rows, ny * width), pltpu.VMEM((a_rows, ny * width), F32),
            dma(8),
            dma(GROUP), dma(GROUP), dma(GROUP), dma(GROUP), dma(GROUP), dma(GROUP),
            dma(nz), dma(nz), dma(nz), dma(nz), dma(nz), dma(nz),
            dma(ny, GROUP), dma(ny, GROUP), dma(ny, GROUP), dma(ny, GROUP),
        ],
        compiler_params=pltpu.CompilerParams(
            collective_id=0, has_side_effects=True, vmem_limit_bytes=56 * 1024 * 1024
        ),
        name="cross_attention",
    )(vl, al, vq, vk, vv, aq, ak, av, wv, wa)


def solution(mesh):
    nz = mesh.shape["seq"] // GROUP
    ny = mesh.shape["head"]

    def program(*arrays):
        return per_device(nz, ny, *arrays)

    return jax.shard_map(
        program,
        mesh=mesh,
        in_specs=(*(P("seq", "head"),) * 6, P(), P(), P(None, "head"), P(None, "head")),
        out_specs=(P("seq", "head"), P("seq", "head")),
        check_vma=False,
    )
```

time: 136 us -> 48.6 us (0.36)
  the two profiles are of different devices: /device:TPU:2 before, /device:TPU:1 now
where the time goes in v1:
time: 48.6 us; the launch traced here: 48.4 us
  Pallas kernels  44.8 us (92%)
  local copies, waits for them, and re-layouts  2.96 us (6%)
  between operations  0.64 us (1%)
    pallas_call x1, Pallas kernels, per_device(): pl.pallas_call(body, out_shape=(jax.ShapeDtypeStruct((rows, wv.shape[1]),...  44.8 us
    unnamed x2, local copies, waits for them, and re-layouts  2.96 us

profile of v1, /device:TPU:1, one launch (start us, length us, event | category | flops | bytes accessed | tf_op | source)
XLA Modules:
  0.0 48.4 jit_solution(10443965127094789035)
XLA Ops:
  0.6 44.8 %cross_attention.1 = (bf16[128,1024]{1,0:T(8,128)(2,1)}, bf16[8,512]{1,0:T(8,128)(2,1)}) custom-call(s32[4]{0:T(128)} %refs_0_.1, s32[4]{0:T(128)} %refs_1_.1, bf16[128,512]{1,0:T(8,128)(2,1)} %refs_2_.1, bf16[128,512]{1,0:T(8,128)(2,1)} %refs_3_.1, bf16[128,512]{1,0:T(8,128)(2,1)} %refs_4_.1, bf16[8,512]{1,0:T(8,128)(2,1)} %refs_5_.1, ...), custom_call_target="tpu_custom_call" | custom-call | tf_op jit(solution)/shard_map/cross_attention/pallas_call | solution.py:398
  45.5 1.7 %copy.14 = bf16[128,1024]{1,0:T(8,128)(2,1)} copy(bf16[128,1024]{1,0:T(8,128)(2,1)} %get-tuple-element.4) | data formatting | bytes 524288
  47.1 1.3 %copy.15 = bf16[8,512]{1,0:T(8,128)(2,1)} copy(bf16[8,512]{1,0:T(8,128)(2,1)} %get-tuple-element.5) | data formatting | bytes 16384

commit v2 on v1

v2 whole, which is shorter than its diff:
```python
import math

import jax
import jax.numpy as jnp
from jax import lax
from jax.experimental import pallas as pl
from jax.experimental.pallas import tpu as pltpu
from jax.sharding import PartitionSpec as P

HEAD_DIM = 64
NX = 4
MESH = pl.DeviceIdType.MESH
BF = jnp.bfloat16
F32 = jnp.float32
FORBID = -65536.0
LOG2E = math.log2(math.e)
SCALE = LOG2E / math.sqrt(HEAD_DIM)


def nt_dot(a, b):
    return lax.dot_general(a, b, (((1,), (1,)), ((), ())), preferred_element_type=F32)


def nn_dot(a, b):
    return lax.dot_general(a, b, (((1,), (0,)), ((), ())), preferred_element_type=F32)


def swap(x):
    return pltpu.roll(x, 64, x.ndim - 1)


def lanes(shape):
    return lax.broadcasted_iota(jnp.int32, shape, len(shape) - 1)


def low(shape):
    return lanes(shape) < 64


def kernel(
    nz, ny,
    vl, al, vq, vk, vv, aq, ak, av, wv_hbm, wa_hbm,
    vo, ao,
    ina_q, ina_k, ina_v, wv, wa,
    tok_aug, aud_aug,
    senda, recva, recvq, kvb, zkv, zq, kk, v0, v1,
    sendo, attn, sendr, recvr, sendx, recvx, sendf, aud,
    in_sem,
    a_s, a_r, q_s, q_r, kv_s, kv_r, zk_s, zk_r, zq_s, zq_r, c_s, c_r, r_s, r_r, o_s, o_r, f_s, f_r,
):
    s = lax.axis_index("seq")
    y = lax.axis_index("head")
    z = s // (2 * NX)
    x = lax.rem(s // 2, NX)
    c = lax.rem(s, 2)
    other = 1 - c
    at = nz * 64
    vt = 2 * NX * 128

    def loop(lo, hi, body):
        def step(i, carry):
            body(i)
            return carry
        lax.fori_loop(lo, hi, step, 0)

    def at_x(d):
        return lax.rem(x + d, NX)

    def at_z(d):
        return lax.rem(z + d, nz)

    def at_y(d):
        return lax.rem(y + d, ny)

    def peer(zz, xx, cc, yy):
        return ((zz * NX + xx) * 2 + cc, yy)

    def remote(src, dst, ss, rs, to):
        return pltpu.make_async_remote_copy(
            src_ref=src, dst_ref=dst, send_sem=ss, recv_sem=rs, device_id=to, device_id_type=MESH
        )

    partner = peer(z, x, other, y)

    def arrived(dst, rs):
        remote(dst, dst, rs, rs, partner).wait_recv()

    def columns(ref, t):
        return ref.at[:, pl.ds(pl.multiple_of(t * 128, 128), 128)]

    local = [
        pltpu.make_async_copy(src, dst, in_sem.at[i])
        for i, (src, dst) in enumerate(
            [
                (aq, ina_q), (ak, ina_k), (av, ina_v),
                (columns(vq, x), recvq.at[x]),
                (columns(vk, x), kvb.at[c, x, 0]),
                (columns(vv, x), kvb.at[c, x, 1]),
                (wv_hbm, wv), (wa_hbm, wa),
            ]
        )
    ]
    for copy in local:
        copy.start()

    barrier = pltpu.get_barrier_semaphore()

    def greet(to):
        pl.semaphore_signal(barrier, inc=1, device_id=to, device_id_type=MESH)

    greet(partner)
    loop(1, nz, lambda d: greet(peer(at_z(d), x, c, y)))
    loop(1, NX * ny, lambda n: greet(peer(z, at_x(lax.rem(n, NX)), c, at_y(n // NX))))

    v_end = [vl[0]]
    a_end = [al[0]]
    for i in range(1, 4):
        v_end.append(v_end[-1] + vl[i])
        a_end.append(a_end[-1] + al[i])

    def clip_of(pos, ends):
        total = jnp.zeros_like(pos)
        for e in ends:
            total = total + (pos >= e).astype(jnp.int32)
        return total

    def iotas(shape):
        return [lax.broadcasted_iota(jnp.int32, shape, i) for i in range(len(shape))]

    core, place, row, lane = iotas((2, NX, 128, 128))
    token = ((z * NX + place) * 2 + core) * 128 + row
    tok_aug[...] = jnp.where(clip_of(token, v_end) == lane, 1.0, 0.0).astype(BF)
    core, slab, row, lane = iotas((2, nz, 32, 128))
    pos = slab * 64 + (row >> 3) * 16 + core * 8 + (row & 7) + at // 2
    pos = jnp.where(pos >= at, pos - at, pos)
    mark = jnp.where((lane < 4) & (clip_of(pos, a_end) != lane), FORBID, 0.0).astype(BF)
    aud_aug[...] = mark
    kk[0:at, 128:256] = mark.reshape(at, 128)
    kk[at : 2 * at, 128:256] = mark.reshape(at, 128)

    for i in range(3):
        local[i].wait()
    for p in range(NX):
        cols = pl.ds(128 * p, 128)
        k8, v8, q8 = (r[:, cols].astype(F32) for r in (ina_k, ina_v, ina_q))
        senda[p] = jnp.concatenate([k8, v8, q8, q8], axis=0).astype(BF)

    pl.semaphore_wait(barrier, 1 + nz - 1 + NX * ny - 1)

    def a_copy(d):
        t = at_x(d)
        return remote(senda.at[t], recva.at[x], a_s.at[t], a_r.at[x], peer(z, t, c, y))

    def q_copy(d):
        t = at_x(d)
        return remote(columns(vq, t), recvq.at[x], q_s.at[t], q_r.at[x], peer(z, t, c, y))

    def k_copy(d):
        t = at_x(d)
        return remote(columns(vk, t), kvb.at[c, x, 0], kv_s.at[0, t], kv_r.at[0, x], peer(z, t, c, y))

    def v_copy(d):
        t = at_x(d)
        return remote(columns(vv, t), kvb.at[c, x, 1], kv_s.at[1, t], kv_r.at[1, x], peer(z, t, c, y))

    for copy in (a_copy, q_copy, k_copy, v_copy):
        for d in range(1, NX):
            copy(d).start()

    recva[x] = senda[x]

    for d in range(1, NX):
        arrived(recva.at[at_x(d)], a_r.at[at_x(d)])
    got = recva[...].astype(F32)
    zkv[c, z] = jnp.concatenate([got[:, 0:8].reshape(32, 128), got[:, 8:16].reshape(32, 128)], axis=0).astype(BF)
    zq[c, z] = got[:, 16:24].reshape(32, 128).astype(BF)

    def zk_copy(d):
        t = at_z(d)
        return remote(zkv.at[c, z], zkv.at[c, z], zk_s.at[t], zk_r.at[z], peer(t, x, c, y))

    def zq_copy(d):
        t = at_z(d)
        return remote(zq.at[c, z], zq.at[c, z], zq_s.at[t], zq_r.at[z], peer(t, x, c, y))

    loop(1, nz, lambda d: zk_copy(d).start())
    loop(1, nz, lambda d: zq_copy(d).start())
    loop(1, nz, lambda d: arrived(zkv.at[c, at_z(d)], zk_r.at[at_z(d)]))

    zk_share = remote(zkv.at[c], zkv.at[c], c_s.at[0], c_r.at[0], partner)
    zq_share = remote(zq.at[c], zq.at[c], c_s.at[1], c_r.at[1], partner)
    kv_share = remote(kvb.at[c], kvb.at[c], c_s.at[2], c_r.at[2], partner)
    zk_share.start()
    local[3].wait()
    for d in range(1, NX):
        arrived(recvq.at[at_x(d)], q_r.at[at_x(d)])
    arrived(zkv.at[other], c_r.at[0])

    low_at = low((at, 128))
    key = zkv[:, :, 0:32].reshape(at, 128).astype(F32)
    kk[0:at, 0:128] = jnp.where(low_at, key, 0.0).astype(BF)
    kk[at : 2 * at, 0:128] = jnp.where(low_at, 0.0, key).astype(BF)
    value = zkv[:, :, 32:64].reshape(at, 128).astype(F32)
    v0[0:at] = jnp.where(low_at, value, 1.0).astype(BF)
    v1[...] = jnp.where(low_at, 1.0, value).astype(BF)

    low128 = low((128, 128))

    def o_copy(t, e):
        u = at_y(e)
        return remote(sendo.at[t], attn.at[y, x], o_s.at[u, t], o_r.at[y, x], peer(z, t, c, u))

    def video_block(t):
        query = jnp.concatenate([recvq[t], tok_aug[c, t]], axis=1)
        sc = nt_dot(query, kk[...])
        outs = []
        for half, values in ((sc[:, 0:at], v0[0:at]), (sc[:, at : 2 * at], v1[...])):
            top = jnp.max(half, axis=1, keepdims=True)
            w = jnp.exp2((half - top) * SCALE).astype(BF)
            outs.append(nn_dot(w, values))
        num = jnp.where(low128, outs[0], outs[1])
        den = swap(jnp.where(low128, outs[1], outs[0]))
        return (num / den).astype(BF)

    for d in range(1, NX):
        t = at_x(d)
        sendo[t] = video_block(t)
        for e in range(ny):
            o_copy(t, e).start()
        if d == 2:
            for i in (4, 5):
                local[i].wait()
            for n in range(1, NX):
                for i in range(2):
                    arrived(kvb.at[c, at_x(n), i], kv_r.at[i, at_x(n)])
            kv_share.start()
            loop(1, nz, lambda n: arrived(zq.at[c, at_z(n)], zq_r.at[at_z(n)]))
            zq_share.start()
    sendo[x] = video_block(x)
    for e in range(1, ny):
        o_copy(x, e).start()
    attn[y, x] = sendo[x]

    arrived(kvb.at[other], c_r.at[2])
    arrived(zq.at[other], c_r.at[1])
    mine_vt = low((vt, 128)) == (c == 0)
    v0[0:vt] = jnp.where(mine_vt, kvb[:, :, 1].reshape(vt, 128).astype(F32), 1.0).astype(BF)
    mine128 = low128 == (c == 0)
    lane128 = lanes((128, 128))

    def audio_block(p):
        query = zq[:, pl.ds(2 * p, 2)].reshape(128, 128).astype(F32)
        query = jnp.where(mine128, query, 0.0).astype(BF)
        query = jnp.concatenate([query, aud_aug[:, pl.ds(2 * p, 2)].reshape(128, 128)], axis=1)
        keys = jnp.concatenate([kvb[:, :, 0].reshape(vt, 128), tok_aug[...].reshape(vt, 128)], axis=1)
        sc = nt_dot(query, keys)
        top = jnp.max(sc, axis=1, keepdims=True)
        w = jnp.exp2((sc - top) * SCALE).astype(BF)
        full = nn_dot(w, v0[0:vt])
        turned = swap(full)
        full, turned = jnp.where(c == 0, full, turned), jnp.where(c == 0, turned, full)
        mean = full / turned
        level = top * SCALE + jnp.log(jnp.where(low128, 1.0, full)) * LOG2E
        first = level.astype(BF).astype(F32)
        second = (level - first).astype(BF).astype(F32)
        third = level - first - second
        parts = jnp.where(lane128 < 96, first, jnp.where(lane128 < 112, second, third))
        out = jnp.where(low128, mean, parts).reshape(2, 2, 32, 128)
        return [out[:, i].reshape(64, 128).astype(BF) for i in range(2)]

    def r_copy(t):
        return remote(sendr.at[t], recvr.at[z], r_s.at[t], r_r.at[z], peer(t, x, c, y))

    def audio_step(d):
        p = lax.rem(z // 2 + d, nz // 2)
        done = audio_block(p)
        for i in range(2):
            sendr[2 * p + i] = done[i]
        for i in range(2):
            r_copy(2 * p + i).start()

    loop(1, nz // 2, audio_step)
    pair = z // 2
    near = 2 * pair + (1 - lax.rem(z, 2))
    done = audio_block(pair)
    for i in range(2):
        sendr[2 * pair + i] = done[i]
    r_copy(near).start()
    recvr[z] = sendr[z]

    loop(1, nz, lambda d: arrived(recvr.at[at_z(d)], r_r.at[at_z(d)]))
    part = recvr[...].astype(F32)
    level = part[:, :, 64:65] + part[:, :, 96:97] + part[:, :, 112:113]
    share = jnp.exp2(level - jnp.max(level, axis=0, keepdims=True))
    mixed = jnp.sum(part * share, axis=0) / jnp.sum(share, axis=0)
    mixed = jnp.where(c == 0, mixed, swap(mixed))
    sendx[...] = jnp.where(c == 0, mixed[32:64], mixed[0:32])
    x_share = remote(sendx, recvx, c_s.at[3], c_r.at[3], partner)
    x_share.start()
    arrived(recvx, c_r.at[3])
    mine32 = low((32, 128)) == (c == 0)
    both = jnp.where(mine32, jnp.where(c == 0, mixed[0:32], mixed[32:64]), recvx[...])
    sendf[...] = both.reshape(NX, 8, 128)

    def f_copy(n):
        t = at_x(lax.rem(n, NX))
        u = at_y(n // NX)
        return remote(sendf.at[t], aud.at[y, x], f_s.at[u, t], f_r.at[y, x], peer(z, t, c, u))

    loop(1, NX * ny, lambda n: f_copy(n).start())
    aud[y, x] = sendf[x]

    def wait_o(n):
        t = at_x(lax.rem(n, NX))
        u = at_y(n // NX)
        arrived(attn.at[u, t], o_r.at[u, t])

    loop(1, NX * ny, wait_o)
    every = [(u, t) for u in range(ny) for t in range(NX)]
    local[6].wait()
    hidden = jnp.concatenate([attn[u, t] for u, t in every], axis=1)
    width = wv.shape[1] // 4
    for n in range(4):
        cols = pl.ds(n * width, width)
        vo[:, cols] = nn_dot(hidden, wv[:, cols]).astype(BF)

    def wait_f(n):
        t = at_x(lax.rem(n, NX))
        u = at_y(n // NX)
        arrived(aud.at[u, t], f_r.at[u, t])

    loop(1, NX * ny, wait_f)
    local[7].wait()
    hidden = jnp.concatenate([aud[u, t] for u, t in every], axis=1).astype(BF)
    ao[...] = nn_dot(hidden, wa[...]).astype(BF)

    for copy in (a_copy, q_copy, k_copy, v_copy):
        for d in range(1, NX):
            copy(d).wait_send()
    for copy in (zk_share, zq_share, kv_share, x_share):
        copy.wait_send()

    def sent_ring(d):
        zk_copy(d).wait_send()
        zq_copy(d).wait_send()
        r_copy(at_z(d)).wait_send()

    def sent_out(n):
        o_copy(at_x(lax.rem(n, NX)), n // NX).wait_send()
        f_copy(n).wait_send()

    loop(1, nz, sent_ring)
    loop(1, NX * ny, sent_out)


def per_device(nz, ny, vq, vk, vv, aq, ak, av, vl, al, wv, wa):
    rows, width = vq.shape
    a_rows = aq.shape[0]
    at = nz * 64
    vt = 2 * NX * 128
    hbm = pl.BlockSpec(memory_space=pl.ANY)
    smem = pl.BlockSpec(memory_space=pltpu.SMEM)
    vmem = pl.BlockSpec(memory_space=pltpu.VMEM)
    bf = lambda *shape: pltpu.VMEM(shape, BF)
    wide = lambda *shape: pltpu.VMEM(shape, F32)
    dma = lambda *shape: pltpu.SemaphoreType.DMA(shape)

    def body(*refs):
        kernel(nz, ny, *refs)

    return pl.pallas_call(
        body,
        out_shape=(
            jax.ShapeDtypeStruct((rows, wv.shape[1]), BF),
            jax.ShapeDtypeStruct((a_rows, wa.shape[1]), BF),
        ),
        in_specs=[smem, smem] + [hbm] * 8,
        out_specs=(vmem, vmem),
        scratch_shapes=[
            bf(a_rows, width), bf(a_rows, width), bf(a_rows, width),
            bf(*wv.shape), bf(*wa.shape),
            bf(2, NX, 128, 128), bf(2, nz, 32, 128),
            bf(NX, 32, 128), bf(NX, 32, 128), bf(NX, 128, 128), bf(2, NX, 2, 128, 128),
            bf(2, nz, 64, 128), bf(2, nz, 32, 128),
            bf(2 * at, 256), bf(max(at, vt), 128), bf(at, 128),
            bf(NX, 128, 128), bf(ny, NX, 128, 128),
            bf(nz, 64, 128), bf(nz, 64, 128),
            wide(32, 128), wide(32, 128), wide(NX, 8, 128), wide(ny, NX, 8, 128),
            dma(8),
            dma(NX), dma(NX), dma(NX), dma(NX), dma(2, NX), dma(2, NX),
            dma(nz), dma(nz), dma(nz), dma(nz), dma(4), dma(4), dma(nz), dma(nz),
            dma(ny, NX), dma(ny, NX), dma(ny, NX), dma(ny, NX),
        ],
        compiler_params=pltpu.CompilerParams(
            collective_id=0, has_side_effects=True, vmem_limit_bytes=56 * 1024 * 1024
        ),
        name="cross_attention",
    )(vl, al, vq, vk, vv, aq, ak, av, wv, wa)


def solution(mesh):
    nz = mesh.shape["seq"] // (2 * NX)
    ny = mesh.shape["head"]

    def program(*arrays):
        return per_device(nz, ny, *arrays)

    return jax.shard_map(
        program,
        mesh=mesh,
        in_specs=(*(P("seq", "head"),) * 6, P(), P(), P(None, "head"), P(None, "head")),
        out_specs=(P("seq", "head"), P("seq", "head")),
        check_vma=False,
    )
```

time: 48.6 us -> 43.4 us (0.89)
  Pallas kernels: 44.8 us -> 39.6 us
    pallas_call x1, Pallas kernels: 44.8 us -> 39.6 us  [per_device(): pl.pallas_call(body, out_shape=(jax.ShapeDtypeStruct((rows, wv.shape[1]),...]
where the time goes in v2:
time: 43.4 us; the launch traced here: 43.2 us
  Pallas kernels  39.6 us (91%)
  local copies, waits for them, and re-layouts  2.96 us (7%)
  between operations  0.64 us (1%)
    pallas_call x1, Pallas kernels, per_device(): pl.pallas_call(body, out_shape=(jax.ShapeDtypeStruct((rows, wv.shape[1]),...  39.6 us
    unnamed x2, local copies, waits for them, and re-layouts  2.96 us

profile of v2, /device:TPU:1, one launch (start us, length us, event | category | flops | bytes accessed | tf_op | source)
XLA Modules:
  0.0 43.2 jit_solution(8093125921962690056)
XLA Ops:
  0.6 39.6 %cross_attention.1 = (bf16[128,1024]{1,0:T(8,128)(2,1)}, bf16[8,512]{1,0:T(8,128)(2,1)}) custom-call(s32[4]{0:T(128)} %refs_0_.1, s32[4]{0:T(128)} %refs_1_.1, bf16[128,512]{1,0:T(8,128)(2,1)} %refs_2_.1, bf16[128,512]{1,0:T(8,128)(2,1)} %refs_3_.1, bf16[128,512]{1,0:T(8,128)(2,1)} %refs_4_.1, bf16[8,512]{1,0:T(8,128)(2,1)} %refs_5_.1, ...), custom_call_target="tpu_custom_call" | custom-call | tf_op jit(solution)/shard_map/cross_attention/pallas_call | solution.py:371
  40.3 1.7 %copy.14 = bf16[128,1024]{1,0:T(8,128)(2,1)} copy(bf16[128,1024]{1,0:T(8,128)(2,1)} %get-tuple-element.4) | data formatting | bytes 524288
  41.9 1.3 %copy.15 = bf16[8,512]{1,0:T(8,128)(2,1)} copy(bf16[8,512]{1,0:T(8,128)(2,1)} %get-tuple-element.5) | data formatting | bytes 16384

commit v3 on v2

--- a/solution.py
+++ b/solution.py
@@ -9,6 +9,8 @@
 
 HEAD_DIM = 64
 NX = 4
+VIDEO = [[[1, 2]], [[3, 0]]]
+AUDIO = 2
 MESH = pl.DeviceIdType.MESH
 BF = jnp.bfloat16
 F32 = jnp.float32
@@ -17,10 +19,6 @@
 SCALE = LOG2E / math.sqrt(HEAD_DIM)
 
 
-def nt_dot(a, b):
-    return lax.dot_general(a, b, (((1,), (1,)), ((), ())), preferred_element_type=F32)
-
-
 def nn_dot(a, b):
     return lax.dot_general(a, b, (((1,), (0,)), ((), ())), preferred_element_type=F32)
 
@@ -43,10 +41,10 @@
     vo, ao,
     ina_q, ina_k, ina_v, wv, wa,
     tok_aug, aud_aug,
-    senda, recva, recvq, kvb, zkv, zq, kk, v0, v1,
+    senda, recva, recvq, kvb, zall, ka, kv, v0, v1, vg,
     sendo, attn, sendr, recvr, sendx, recvx, sendf, aud,
     in_sem,
-    a_s, a_r, q_s, q_r, kv_s, kv_r, zk_s, zk_r, zq_s, zq_r, c_s, c_r, r_s, r_r, o_s, o_r, f_s, f_r,
+    a_s, a_r, q_s, q_r, kv_s, kv_r, z_s, z_r, c_s, c_r, r_s, r_r, o_s, o_r, f_s, f_r,
 ):
     s = lax.axis_index("seq")
     y = lax.axis_index("head")
@@ -127,16 +125,25 @@
     def iotas(shape):
         return [lax.broadcasted_iota(jnp.int32, shape, i) for i in range(len(shape))]
 
-    core, place, row, lane = iotas((2, NX, 128, 128))
-    token = ((z * NX + place) * 2 + core) * 128 + row
+    def audio_pos(core, slab, row):
+        pos = slab * 64 + (row >> 3) * 16 + core * 8 + (row & 7) + at // 2
+        return jnp.where(pos >= at, pos - at, pos)
+
+    place, row, lane = iotas((NX, 128, 128))
+    token = ((z * NX + place) * 2 + c) * 128 + row
     tok_aug[...] = jnp.where(clip_of(token, v_end) == lane, 1.0, 0.0).astype(BF)
     core, slab, row, lane = iotas((2, nz, 32, 128))
-    pos = slab * 64 + (row >> 3) * 16 + core * 8 + (row & 7) + at // 2
-    pos = jnp.where(pos >= at, pos - at, pos)
-    mark = jnp.where((lane < 4) & (clip_of(pos, a_end) != lane), FORBID, 0.0).astype(BF)
-    aud_aug[...] = mark
-    kk[0:at, 128:256] = mark.reshape(at, 128)
-    kk[at : 2 * at, 128:256] = mark.reshape(at, 128)
+    forbidden = (lane < 4) & (clip_of(audio_pos(core, slab, row), a_end) != lane)
+    aud_aug[...] = jnp.where(forbidden, FORBID, 0.0).astype(BF)
+    mark, col = iotas((128, NX * 128))
+    for m in range(2):
+        token = (z * NX + (col >> 7)) * 256 + m * 128 + (col & 127)
+        kv[m, 128:256] = jnp.where(clip_of(token, v_end) == mark, 1.0, 0.0).astype(BF)
+    mark, col = iotas((128, nz * 32))
+    for m in range(2):
+        forbidden = (mark < 4) & (clip_of(audio_pos(m, col >> 5, col & 31), a_end) != mark)
+        marks = jnp.where(forbidden, FORBID, 0.0).astype(BF)
+        ka[m, 128:256] = jnp.concatenate([marks, marks], axis=1)
 
     for i in range(3):
         local[i].wait()
@@ -163,7 +170,7 @@
         t = at_x(d)
         return remote(columns(vv, t), kvb.at[c, x, 1], kv_s.at[1, t], kv_r.at[1, x], peer(z, t, c, y))
 
-    for copy in (a_copy, q_copy, k_copy, v_copy):
+    for copy in (a_copy, k_copy, v_copy, q_copy):
         for d in range(1, NX):
             copy(d).start()
 
@@ -172,37 +179,58 @@
     for d in range(1, NX):
         arrived(recva.at[at_x(d)], a_r.at[at_x(d)])
     got = recva[...].astype(F32)
-    zkv[c, z] = jnp.concatenate([got[:, 0:8].reshape(32, 128), got[:, 8:16].reshape(32, 128)], axis=0).astype(BF)
-    zq[c, z] = got[:, 16:24].reshape(32, 128).astype(BF)
-
-    def zk_copy(d):
+    rows = [got[:, 8 * i : 8 * i + 8].reshape(32, 128) for i in range(3)]
+    zall[c, z] = jnp.concatenate(rows, axis=0).astype(BF)
+
+    def z_copy(d):
         t = at_z(d)
-        return remote(zkv.at[c, z], zkv.at[c, z], zk_s.at[t], zk_r.at[z], peer(t, x, c, y))
-
-    def zq_copy(d):
-        t = at_z(d)
-        return remote(zq.at[c, z], zq.at[c, z], zq_s.at[t], zq_r.at[z], peer(t, x, c, y))
-
-    loop(1, nz, lambda d: zk_copy(d).start())
-    loop(1, nz, lambda d: zq_copy(d).start())
-    loop(1, nz, lambda d: arrived(zkv.at[c, at_z(d)], zk_r.at[at_z(d)]))
-
-    zk_share = remote(zkv.at[c], zkv.at[c], c_s.at[0], c_r.at[0], partner)
-    zq_share = remote(zq.at[c], zq.at[c], c_s.at[1], c_r.at[1], partner)
-    kv_share = remote(kvb.at[c], kvb.at[c], c_s.at[2], c_r.at[2], partner)
-    zk_share.start()
+        return remote(zall.at[c, z], zall.at[c, z], z_s.at[t], z_r.at[z], peer(t, x, c, y))
+
+    for d in range(1, nz):
+        z_copy(d).start()
+
+    z_share = remote(zall.at[c], zall.at[c], c_s.at[0], c_r.at[0], partner)
+    kv_share = remote(kvb.at[c], kvb.at[c], c_s.at[1], c_r.at[1], partner)
+    for i in (4, 5):
+        local[i].wait()
+    for n in range(1, NX):
+        for i in range(2):
+            arrived(kvb.at[c, at_x(n), i], kv_r.at[i, at_x(n)])
+    kv_share.start()
+    for d in range(1, nz):
+        arrived(zall.at[c, at_z(d)], z_r.at[at_z(d)])
+    z_share.start()
+
+    low_row = low((1, 128))
+    head0 = jnp.where(low_row, 1.0, 0.0).astype(BF)
+    head1 = jnp.where(low_row, 0.0, 1.0).astype(BF)
+    mine = jnp.where(c == 0, head0.astype(F32), head1.astype(F32)).astype(BF)
+    rest = jnp.where(c == 0, head1.astype(F32), head0.astype(F32)).astype(BF)
+    half_at = at // 2
+    upper = lax.broadcasted_iota(jnp.int32, (128, half_at), 0) < 64
+
+    def prepare_audio(m):
+        rows = pl.ds(pl.multiple_of(m * half_at, half_at), half_at)
+        key = zall[m, :, 0:32].reshape(half_at, 128).astype(F32).T
+        ka[m, 0:128] = jnp.concatenate([jnp.where(upper, key, 0.0), jnp.where(upper, 0.0, key)], axis=1).astype(BF)
+        value = zall[m, :, 32:64].reshape(half_at, 128)
+        v0[rows] = value * head0 + head1
+        v1[rows] = value * head1 + head0
+
+    def prepare_video(m):
+        rows = pl.ds(pl.multiple_of(m * (vt // 2), vt // 2), vt // 2)
+        kv[m, 0:128] = kvb[m, :, 0].reshape(vt // 2, 128).astype(F32).T.astype(BF)
+        vg[rows] = kvb[m, :, 1].reshape(vt // 2, 128) * mine + rest
+
+    prepare_video(c)
+    prepare_audio(c)
     local[3].wait()
     for d in range(1, NX):
         arrived(recvq.at[at_x(d)], q_r.at[at_x(d)])
-    arrived(zkv.at[other], c_r.at[0])
-
-    low_at = low((at, 128))
-    key = zkv[:, :, 0:32].reshape(at, 128).astype(F32)
-    kk[0:at, 0:128] = jnp.where(low_at, key, 0.0).astype(BF)
-    kk[at : 2 * at, 0:128] = jnp.where(low_at, 0.0, key).astype(BF)
-    value = zkv[:, :, 32:64].reshape(at, 128).astype(F32)
-    v0[0:at] = jnp.where(low_at, value, 1.0).astype(BF)
-    v1[...] = jnp.where(low_at, 1.0, value).astype(BF)
+    arrived(kvb.at[other], c_r.at[1])
+    prepare_video(other)
+    arrived(zall.at[other], c_r.at[0])
+    prepare_audio(other)
 
     low128 = low((128, 128))
 
@@ -211,10 +239,11 @@
         return remote(sendo.at[t], attn.at[y, x], o_s.at[u, t], o_r.at[y, x], peer(z, t, c, u))
 
     def video_block(t):
-        query = jnp.concatenate([recvq[t], tok_aug[c, t]], axis=1)
-        sc = nt_dot(query, kk[...])
+        query = jnp.concatenate([recvq[t], tok_aug[t]], axis=1)
+        scs = [nn_dot(query, ka[m]) for m in range(2)]
         outs = []
-        for half, values in ((sc[:, 0:at], v0[0:at]), (sc[:, at : 2 * at], v1[...])):
+        for i, values in ((0, v0[...]), (1, v1[...])):
+            half = jnp.concatenate([sc[:, i * half_at : (i + 1) * half_at] for sc in scs], axis=1)
             top = jnp.max(half, axis=1, keepdims=True)
             w = jnp.exp2((half - top) * SCALE).astype(BF)
             outs.append(nn_dot(w, values))
@@ -222,41 +251,23 @@
         den = swap(jnp.where(low128, outs[1], outs[0]))
         return (num / den).astype(BF)
 
-    for d in range(1, NX):
-        t = at_x(d)
-        sendo[t] = video_block(t)
-        for e in range(ny):
-            o_copy(t, e).start()
-        if d == 2:
-            for i in (4, 5):
-                local[i].wait()
-            for n in range(1, NX):
-                for i in range(2):
-                    arrived(kvb.at[c, at_x(n), i], kv_r.at[i, at_x(n)])
-            kv_share.start()
-            loop(1, nz, lambda n: arrived(zq.at[c, at_z(n)], zq_r.at[at_z(n)]))
-            zq_share.start()
-    sendo[x] = video_block(x)
-    for e in range(1, ny):
-        o_copy(x, e).start()
-    attn[y, x] = sendo[x]
-
-    arrived(kvb.at[other], c_r.at[2])
-    arrived(zq.at[other], c_r.at[1])
-    mine_vt = low((vt, 128)) == (c == 0)
-    v0[0:vt] = jnp.where(mine_vt, kvb[:, :, 1].reshape(vt, 128).astype(F32), 1.0).astype(BF)
-    mine128 = low128 == (c == 0)
+    def video_steps(ds):
+        done = [video_block(at_x(d)) for d in ds]
+        for d, block in zip(ds, done):
+            sendo[at_x(d)] = block
+        for d in ds:
+            for e in range(ny) if d else range(1, ny):
+                o_copy(at_x(d), e).start()
+
     lane128 = lanes((128, 128))
 
     def audio_block(p):
-        query = zq[:, pl.ds(2 * p, 2)].reshape(128, 128).astype(F32)
-        query = jnp.where(mine128, query, 0.0).astype(BF)
+        query = zall[:, pl.ds(2 * p, 2), 64:96].reshape(128, 128) * mine
         query = jnp.concatenate([query, aud_aug[:, pl.ds(2 * p, 2)].reshape(128, 128)], axis=1)
-        keys = jnp.concatenate([kvb[:, :, 0].reshape(vt, 128), tok_aug[...].reshape(vt, 128)], axis=1)
-        sc = nt_dot(query, keys)
+        sc = jnp.concatenate([nn_dot(query, kv[m]) for m in range(2)], axis=1)
         top = jnp.max(sc, axis=1, keepdims=True)
         w = jnp.exp2((sc - top) * SCALE).astype(BF)
-        full = nn_dot(w, v0[0:vt])
+        full = nn_dot(w, vg[...])
         turned = swap(full)
         full, turned = jnp.where(c == 0, full, turned), jnp.where(c == 0, turned, full)
         mean = full / turned
@@ -271,22 +282,28 @@
     def r_copy(t):
         return remote(sendr.at[t], recvr.at[z], r_s.at[t], r_r.at[z], peer(t, x, c, y))
 
-    def audio_step(d):
-        p = lax.rem(z // 2 + d, nz // 2)
-        done = audio_block(p)
-        for i in range(2):
-            sendr[2 * p + i] = done[i]
-        for i in range(2):
-            r_copy(2 * p + i).start()
-
-    loop(1, nz // 2, audio_step)
-    pair = z // 2
-    near = 2 * pair + (1 - lax.rem(z, 2))
-    done = audio_block(pair)
-    for i in range(2):
-        sendr[2 * pair + i] = done[i]
-    r_copy(near).start()
+    def audio_steps(ds):
+        ps = [lax.rem(z // 2 + d, nz // 2) for d in ds]
+        done = [audio_block(p) for p in ps]
+        for p, blocks in zip(ps, done):
+            for i in range(2):
+                sendr[2 * p + i] = blocks[i]
+        for d, p in zip(ds, ps):
+            if d:
+                for i in range(2):
+                    r_copy(2 * p + i).start()
+            else:
+                r_copy(2 * p + 1 - lax.rem(z, 2)).start()
+
+    pairs = list(range(1, nz // 2)) + [0]
+    for ds in VIDEO[0]:
+        video_steps(ds)
+    for i in range(0, len(pairs), AUDIO):
+        audio_steps(pairs[i : i + AUDIO])
     recvr[z] = sendr[z]
+    for ds in VIDEO[1]:
+        video_steps(ds)
+    attn[y, x] = sendo[x]
 
     loop(1, nz, lambda d: arrived(recvr.at[at_z(d)], r_r.at[at_z(d)]))
     part = recvr[...].astype(F32)
@@ -295,9 +312,9 @@
     mixed = jnp.sum(part * share, axis=0) / jnp.sum(share, axis=0)
     mixed = jnp.where(c == 0, mixed, swap(mixed))
     sendx[...] = jnp.where(c == 0, mixed[32:64], mixed[0:32])
-    x_share = remote(sendx, recvx, c_s.at[3], c_r.at[3], partner)
+    x_share = remote(sendx, recvx, c_s.at[2], c_r.at[2], partner)
     x_share.start()
-    arrived(recvx, c_r.at[3])
+    arrived(recvx, c_r.at[2])
     mine32 = low((32, 128)) == (c == 0)
     both = jnp.where(mine32, jnp.where(c == 0, mixed[0:32], mixed[32:64]), recvx[...])
     sendf[...] = both.reshape(NX, 8, 128)
@@ -309,6 +326,19 @@
 
     loop(1, NX * ny, lambda n: f_copy(n).start())
     aud[y, x] = sendf[x]
+
+    for copy in (a_copy, k_copy, v_copy, q_copy):
+        for d in range(1, NX):
+            copy(d).wait_send()
+    for copy in (z_share, kv_share, x_share):
+        copy.wait_send()
+
+    def sent_ring(d):
+        z_copy(d).wait_send()
+        r_copy(at_z(d)).wait_send()
+
+    loop(1, nz, sent_ring)
+    loop(1, NX * ny, lambda n: o_copy(at_x(lax.rem(n, NX)), n // NX).wait_send())
 
     def wait_o(n):
         t = at_x(lax.rem(n, NX))
@@ -334,23 +364,15 @@
     hidden = jnp.concatenate([aud[u, t] for u, t in every], axis=1).astype(BF)
     ao[...] = nn_dot(hidden, wa[...]).astype(BF)
 
-    for copy in (a_copy, q_copy, k_copy, v_copy):
-        for d in range(1, NX):
-            copy(d).wait_send()
-    for copy in (zk_share, zq_share, kv_share, x_share):
-        copy.wait_send()
-
-    def sent_ring(d):
-        zk_copy(d).wait_send()
-        zq_copy(d).wait_send()
-        r_copy(at_z(d)).wait_send()
-
-    def sent_out(n):
-        o_copy(at_x(lax.rem(n, NX)), n // NX).wait_send()
-        f_copy(n).wait_send()
-
-    loop(1, nz, sent_ring)
-    loop(1, NX * ny, sent_out)
+    loop(1, NX * ny, lambda n: f_copy(n).wait_send())
+
+
+def write_out(v_in, a_in, v_out, a_out, sem):
+    copies = [pltpu.make_async_copy(v_in, v_out, sem.at[0]), pltpu.make_async_copy(a_in, a_out, sem.at[1])]
+    for copy in copies:
+        copy.start()
+    for copy in copies:
+        copy.wait()
 
 
 def per_device(nz, ny, vq, vk, vv, aq, ak, av, vl, al, wv, wa):
@@ -368,27 +390,27 @@
     def body(*refs):
         kernel(nz, ny, *refs)
 
-    return pl.pallas_call(
+    made = pl.pallas_call(
         body,
         out_shape=(
-            jax.ShapeDtypeStruct((rows, wv.shape[1]), BF),
-            jax.ShapeDtypeStruct((a_rows, wa.shape[1]), BF),
+            pltpu.VMEM((rows, wv.shape[1]), BF),
+            pltpu.VMEM((a_rows, wa.shape[1]), BF),
         ),
         in_specs=[smem, smem] + [hbm] * 8,
         out_specs=(vmem, vmem),
         scratch_shapes=[
             bf(a_rows, width), bf(a_rows, width), bf(a_rows, width),
             bf(*wv.shape), bf(*wa.shape),
-            bf(2, NX, 128, 128), bf(2, nz, 32, 128),
+            bf(NX, 128, 128), bf(2, nz, 32, 128),
             bf(NX, 32, 128), bf(NX, 32, 128), bf(NX, 128, 128), bf(2, NX, 2, 128, 128),
-            bf(2, nz, 64, 128), bf(2, nz, 32, 128),
-            bf(2 * at, 256), bf(max(at, vt), 128), bf(at, 128),
+            bf(2, nz, 96, 128),
+            bf(2, 256, at), bf(2, 256, vt // 2), bf(at, 128), bf(at, 128), bf(vt, 128),
             bf(NX, 128, 128), bf(ny, NX, 128, 128),
             bf(nz, 64, 128), bf(nz, 64, 128),
             wide(32, 128), wide(32, 128), wide(NX, 8, 128), wide(ny, NX, 8, 128),
             dma(8),
             dma(NX), dma(NX), dma(NX), dma(NX), dma(2, NX), dma(2, NX),
-            dma(nz), dma(nz), dma(nz), dma(nz), dma(4), dma(4), dma(nz), dma(nz),
+            dma(nz), dma(nz), dma(3), dma(3), dma(nz), dma(nz),
             dma(ny, NX), dma(ny, NX), dma(ny, NX), dma(ny, NX),
         ],
         compiler_params=pltpu.CompilerParams(
@@ -396,6 +418,15 @@
         ),
         name="cross_attention",
     )(vl, al, vq, vk, vv, aq, ak, av, wv, wa)
+    shapes = (jax.ShapeDtypeStruct((rows, wv.shape[1]), BF), jax.ShapeDtypeStruct((a_rows, wa.shape[1]), BF))
+    return pl.pallas_call(
+        write_out,
+        out_shape=shapes,
+        in_specs=[vmem, vmem],
+        out_specs=(hbm, hbm),
+        scratch_shapes=[dma(2)],
+        name="write_out",
+    )(*(pltpu.with_memory_space_constraint(m, pltpu.VMEM) for m in made))
 
 
 def solution(mesh):

time: 43.4 us -> 37.9 us (0.87)
  local copies, waits for them, and re-layouts: 2.96 us -> 0 us
  Pallas kernels: 39.6 us -> 37.1 us
    unnamed x2 -> x0, local copies, waits for them, and re-layouts: 2.96 us -> none
    pallas_call x1 -> x2, Pallas kernels: 39.6 us -> 37.1 us  [the longest x1 36.4 us: per_device(): pl.pallas_call(body, out_shape=(pltpu.VMEM((rows, wv.shape[1]), BF), pltp...]
where the time goes in v3:
time: 37.9 us; the launch traced here: 37.8 us
  Pallas kernels  37.1 us (98%)
  between operations  0.64 us (2%)
    pallas_call x1, Pallas kernels, per_device(): pl.pallas_call(body, out_shape=(pltpu.VMEM((rows, wv.shape[1]), BF), pltp...  36.4 us

profile of v3, /device:TPU:1, one launch (start us, length us, event | category | flops | bytes accessed | tf_op | source)
XLA Modules:
  0.0 37.8 jit_solution(5145954077236771501)
XLA Ops:
  0.6 36.4 %cross_attention.1 = (bf16[128,1024]{1,0:T(8,128)(2,1)S(1)}, bf16[8,512]{1,0:T(8,128)(2,1)S(1)}) custom-call(s32[4]{0:T(128)} %refs_0_.1, s32[4]{0:T(128)} %refs_1_.1, bf16[128,512]{1,0:T(8,128)(2,1)} %refs_2_.1, bf16[128,512]{1,0:T(8,128)(2,1)} %refs_3_.1, bf16[128,512]{1,0:T(8,128)(2,1)} %refs_4_.1, bf16[8,512]{1,0:T(8,128)(2,1)} %refs_5_.1, ...), custom_call_target="tpu_custom_call" | custom-call | tf_op jit(solution)/shard_map/cross_attention/pallas_call | solution.py:393
  37.1 0.7 %write_out.1 = (bf16[128,1024]{1,0:T(8,128)(2,1)}, bf16[8,512]{1,0:T(8,128)(2,1)}) custom-call(bf16[128,1024]{1,0:T(8,128)(2,1)S(1)} %get-tuple-element.4.v_in, bf16[8,512]{1,0:T(8,128)(2,1)S(1)} %get-tuple-element.5.a_in), custom_call_target="tpu_custom_call" | custom-call | tf_op jit(solution)/shard_map/write_out/pallas_call | solution.py:422

commit v4 on v3

--- a/solution.py
+++ b/solution.py
@@ -42,7 +42,7 @@
     ina_q, ina_k, ina_v, wv, wa,
     tok_aug, aud_aug,
     senda, recva, recvq, kvb, zall, ka, kv, v0, v1, vg,
-    sendo, attn, sendr, recvr, sendx, recvx, sendf, aud,
+    sendo, attn, sendr, recvr, sendf, aud,
     in_sem,
     a_s, a_r, q_s, q_r, kv_s, kv_r, z_s, z_r, c_s, c_r, r_s, r_r, o_s, o_r, f_s, f_r,
 ):
@@ -56,10 +56,8 @@
     vt = 2 * NX * 128
 
     def loop(lo, hi, body):
-        def step(i, carry):
+        for i in range(lo, hi):
             body(i)
-            return carry
-        lax.fori_loop(lo, hi, step, 0)
 
     def at_x(d):
         return lax.rem(x + d, NX)
@@ -98,7 +96,7 @@
             ]
         )
     ]
-    for copy in local:
+    for copy in local[:6]:
         copy.start()
 
     barrier = pltpu.get_barrier_semaphore()
@@ -106,9 +104,13 @@
     def greet(to):
         pl.semaphore_signal(barrier, inc=1, device_id=to, device_id_type=MESH)
 
+    for d in range(1, NX):
+        greet(peer(z, at_x(d), c, y))
+    for d in sorted(range(1, nz), key=lambda d: abs(d - nz // 2)):
+        greet(peer(at_z(d), x, c, y))
     greet(partner)
-    loop(1, nz, lambda d: greet(peer(at_z(d), x, c, y)))
-    loop(1, NX * ny, lambda n: greet(peer(z, at_x(lax.rem(n, NX)), c, at_y(n // NX))))
+    for d in range(1, ny):
+        greet(peer(z, x, c, at_y(d)))
 
     v_end = [vl[0]]
     a_end = [al[0]]
@@ -152,7 +154,7 @@
         k8, v8, q8 = (r[:, cols].astype(F32) for r in (ina_k, ina_v, ina_q))
         senda[p] = jnp.concatenate([k8, v8, q8, q8], axis=0).astype(BF)
 
-    pl.semaphore_wait(barrier, 1 + nz - 1 + NX * ny - 1)
+    pl.semaphore_wait(barrier, 1 + nz - 1 + NX - 1 + ny - 1)
 
     def a_copy(d):
         t = at_x(d)
@@ -174,6 +176,8 @@
         for d in range(1, NX):
             copy(d).start()
 
+    for copy in local[6:]:
+        copy.start()
     recva[x] = senda[x]
 
     for d in range(1, NX):
@@ -186,7 +190,7 @@
         t = at_z(d)
         return remote(zall.at[c, z], zall.at[c, z], z_s.at[t], z_r.at[z], peer(t, x, c, y))
 
-    for d in range(1, nz):
+    for d in sorted(range(1, nz), key=lambda d: abs(d - nz // 2)):
         z_copy(d).start()
 
     z_share = remote(zall.at[c], zall.at[c], c_s.at[0], c_r.at[0], partner)
@@ -276,51 +280,49 @@
         second = (level - first).astype(BF).astype(F32)
         third = level - first - second
         parts = jnp.where(lane128 < 96, first, jnp.where(lane128 < 112, second, third))
-        out = jnp.where(low128, mean, parts).reshape(2, 2, 32, 128)
-        return [out[:, i].reshape(64, 128).astype(BF) for i in range(2)]
-
-    def r_copy(t):
-        return remote(sendr.at[t], recvr.at[z], r_s.at[t], r_r.at[z], peer(t, x, c, y))
+        return jnp.where(low128, mean, parts).reshape(2, 2, 32, 128).astype(BF)
+
+    def r_copy(t, m):
+        return remote(sendr.at[m, t], recvr.at[c, z], r_s.at[m, t], r_r.at[c, z], peer(t, x, m, y))
 
     def audio_steps(ds):
         ps = [lax.rem(z // 2 + d, nz // 2) for d in ds]
         done = [audio_block(p) for p in ps]
         for p, blocks in zip(ps, done):
-            for i in range(2):
-                sendr[2 * p + i] = blocks[i]
+            sendr[:, pl.ds(2 * p, 2)] = blocks
         for d, p in zip(ds, ps):
-            if d:
-                for i in range(2):
-                    r_copy(2 * p + i).start()
-            else:
-                r_copy(2 * p + 1 - lax.rem(z, 2)).start()
+            for m in range(2):
+                if d:
+                    for i in range(2):
+                        r_copy(2 * p + i, m).start()
+                else:
+                    r_copy(2 * p + 1 - lax.rem(z, 2), m).start()
+            if d == 0:
+                r_copy(z, other).start()
 
     pairs = list(range(1, nz // 2)) + [0]
     for ds in VIDEO[0]:
         video_steps(ds)
     for i in range(0, len(pairs), AUDIO):
         audio_steps(pairs[i : i + AUDIO])
-    recvr[z] = sendr[z]
+    recvr[c, z] = sendr[c, z]
     for ds in VIDEO[1]:
         video_steps(ds)
     attn[y, x] = sendo[x]
 
-    loop(1, nz, lambda d: arrived(recvr.at[at_z(d)], r_r.at[at_z(d)]))
+    arrived(recvr.at[other, z], r_r.at[other, z])
+    for d in range(1, nz):
+        for m in range(2):
+            arrived(recvr.at[m, at_z(d)], r_r.at[m, at_z(d)])
     part = recvr[...].astype(F32)
-    level = part[:, :, 64:65] + part[:, :, 96:97] + part[:, :, 112:113]
-    share = jnp.exp2(level - jnp.max(level, axis=0, keepdims=True))
-    mixed = jnp.sum(part * share, axis=0) / jnp.sum(share, axis=0)
-    mixed = jnp.where(c == 0, mixed, swap(mixed))
-    sendx[...] = jnp.where(c == 0, mixed[32:64], mixed[0:32])
-    x_share = remote(sendx, recvx, c_s.at[2], c_r.at[2], partner)
-    x_share.start()
-    arrived(recvx, c_r.at[2])
-    mine32 = low((32, 128)) == (c == 0)
-    both = jnp.where(mine32, jnp.where(c == 0, mixed[0:32], mixed[32:64]), recvx[...])
+    level = part[:, :, :, 64:65] + part[:, :, :, 96:97] + part[:, :, :, 112:113]
+    share = jnp.exp2(level - jnp.max(level, axis=1, keepdims=True))
+    mixed = jnp.sum(part * share, axis=1) / jnp.sum(share, axis=1)
+    both = jnp.where(low((32, 128)), mixed[0], swap(mixed[1]))
     sendf[...] = both.reshape(NX, 8, 128)
 
     def f_copy(n):
-        t = at_x(lax.rem(n, NX))
+        t = at_x(n % NX)
         u = at_y(n // NX)
         return remote(sendf.at[t], aud.at[y, x], f_s.at[u, t], f_r.at[y, x], peer(z, t, c, u))
 
@@ -330,18 +332,20 @@
     for copy in (a_copy, k_copy, v_copy, q_copy):
         for d in range(1, NX):
             copy(d).wait_send()
-    for copy in (z_share, kv_share, x_share):
+    for copy in (z_share, kv_share):
         copy.wait_send()
 
     def sent_ring(d):
         z_copy(d).wait_send()
-        r_copy(at_z(d)).wait_send()
+        for m in range(2):
+            r_copy(at_z(d), m).wait_send()
 
     loop(1, nz, sent_ring)
-    loop(1, NX * ny, lambda n: o_copy(at_x(lax.rem(n, NX)), n // NX).wait_send())
+    r_copy(z, other).wait_send()
+    loop(1, NX * ny, lambda n: o_copy(at_x(n % NX), n // NX).wait_send())
 
     def wait_o(n):
-        t = at_x(lax.rem(n, NX))
+        t = at_x(n % NX)
         u = at_y(n // NX)
         arrived(attn.at[u, t], o_r.at[u, t])
 
@@ -355,7 +359,7 @@
         vo[:, cols] = nn_dot(hidden, wv[:, cols]).astype(BF)
 
     def wait_f(n):
-        t = at_x(lax.rem(n, NX))
+        t = at_x(n % NX)
         u = at_y(n // NX)
         arrived(aud.at[u, t], f_r.at[u, t])
 
@@ -406,11 +410,11 @@
             bf(2, nz, 96, 128),
             bf(2, 256, at), bf(2, 256, vt // 2), bf(at, 128), bf(at, 128), bf(vt, 128),
             bf(NX, 128, 128), bf(ny, NX, 128, 128),
-            bf(nz, 64, 128), bf(nz, 64, 128),
-            wide(32, 128), wide(32, 128), wide(NX, 8, 128), wide(ny, NX, 8, 128),
+            bf(2, nz, 32, 128), bf(2, nz, 32, 128),
+            wide(NX, 8, 128), wide(ny, NX, 8, 128),
             dma(8),
             dma(NX), dma(NX), dma(NX), dma(NX), dma(2, NX), dma(2, NX),
-            dma(nz), dma(nz), dma(3), dma(3), dma(nz), dma(nz),
+            dma(nz), dma(nz), dma(2), dma(2), dma(2, nz), dma(2, nz),
             dma(ny, NX), dma(ny, NX), dma(ny, NX), dma(ny, NX),
         ],
         compiler_params=pltpu.CompilerParams(

time: 37.9 us -> 36.6 us (0.966)
  Pallas kernels: 37.1 us -> 35.8 us
    pallas_call x1, Pallas kernels: 36.4 us -> 35.1 us  [per_device(): pl.pallas_call(body, out_shape=(pltpu.VMEM((rows, wv.shape[1]), BF), pltp...]
where the time goes in v4:
time: 36.6 us; the launch traced here: 36.5 us
  Pallas kernels  35.8 us (98%)
  between operations  0.64 us (2%)
    pallas_call x1, Pallas kernels, per_device(): pl.pallas_call(body, out_shape=(pltpu.VMEM((rows, wv.shape[1]), BF), pltp...  35.1 us

profile of v4, /device:TPU:1, one launch (start us, length us, event | category | flops | bytes accessed | tf_op | source)
XLA Modules:
  0.0 36.5 jit_solution(5003941524390904102)
XLA Ops:
  0.6 35.1 %cross_attention.1 = (bf16[128,1024]{1,0:T(8,128)(2,1)S(1)}, bf16[8,512]{1,0:T(8,128)(2,1)S(1)}) custom-call(s32[4]{0:T(128)} %refs_0_.1, s32[4]{0:T(128)} %refs_1_.1, bf16[128,512]{1,0:T(8,128)(2,1)} %refs_2_.1, bf16[128,512]{1,0:T(8,128)(2,1)} %refs_3_.1, bf16[128,512]{1,0:T(8,128)(2,1)} %refs_4_.1, bf16[8,512]{1,0:T(8,128)(2,1)} %refs_5_.1, ...), custom_call_target="tpu_custom_call" | custom-call | tf_op jit(solution)/shard_map/cross_attention/pallas_call | solution.py:397
  35.7 0.7 %write_out.1 = (bf16[128,1024]{1,0:T(8,128)(2,1)}, bf16[8,512]{1,0:T(8,128)(2,1)}) custom-call(bf16[128,1024]{1,0:T(8,128)(2,1)S(1)} %get-tuple-element.4.v_in, bf16[8,512]{1,0:T(8,128)(2,1)S(1)} %get-tuple-element.5.a_in), custom_call_target="tpu_custom_call" | custom-call | tf_op jit(solution)/shard_map/write_out/pallas_call | solution.py:426

commit v5 on v4

--- a/solution.py
+++ b/solution.py
@@ -201,10 +201,6 @@
         for i in range(2):
             arrived(kvb.at[c, at_x(n), i], kv_r.at[i, at_x(n)])
     kv_share.start()
-    for d in range(1, nz):
-        arrived(zall.at[c, at_z(d)], z_r.at[at_z(d)])
-    z_share.start()
-
     low_row = low((1, 128))
     head0 = jnp.where(low_row, 1.0, 0.0).astype(BF)
     head1 = jnp.where(low_row, 0.0, 1.0).astype(BF)
@@ -227,12 +223,14 @@
         vg[rows] = kvb[m, :, 1].reshape(vt // 2, 128) * mine + rest
 
     prepare_video(c)
+    for d in range(1, nz):
+        arrived(zall.at[c, at_z(d)], z_r.at[at_z(d)])
+    z_share.start()
+
     prepare_audio(c)
     local[3].wait()
     for d in range(1, NX):
         arrived(recvq.at[at_x(d)], q_r.at[at_x(d)])
-    arrived(kvb.at[other], c_r.at[1])
-    prepare_video(other)
     arrived(zall.at[other], c_r.at[0])
     prepare_audio(other)
 
@@ -260,7 +258,7 @@
         for d, block in zip(ds, done):
             sendo[at_x(d)] = block
         for d in ds:
-            for e in range(ny) if d else range(1, ny):
+            for e in sorted(range(0 if d else 1, ny), key=lambda e: abs(e - ny // 2)):
                 o_copy(at_x(d), e).start()
 
     lane128 = lanes((128, 128))
@@ -300,9 +298,11 @@
             if d == 0:
                 r_copy(z, other).start()
 
-    pairs = list(range(1, nz // 2)) + [0]
+    pairs = sorted(range(1, nz // 2), key=lambda d: abs(d - nz // 4)) + [0]
     for ds in VIDEO[0]:
         video_steps(ds)
+    arrived(kvb.at[other], c_r.at[1])
+    prepare_video(other)
     for i in range(0, len(pairs), AUDIO):
         audio_steps(pairs[i : i + AUDIO])
     recvr[c, z] = sendr[c, z]

time: 36.6 us -> 36.1 us (0.986)
  Pallas kernels: 35.8 us -> 35.3 us
    pallas_call x1, Pallas kernels: 35.1 us -> 34.5 us  [per_device(): pl.pallas_call(body, out_shape=(pltpu.VMEM((rows, wv.shape[1]), BF), pltp...]
where the time goes in v5:
time: 36.1 us; the launch traced here: 35.9 us
  Pallas kernels  35.3 us (98%)
  between operations  0.64 us (2%)
    pallas_call x1, Pallas kernels, per_device(): pl.pallas_call(body, out_shape=(pltpu.VMEM((rows, wv.shape[1]), BF), pltp...  34.5 us
    pallas_call x1, Pallas kernels, per_device(): pl.pallas_call(write_out, out_shape=shapes, in_specs=[vmem, vmem], out_sp...  0.72 us

profile of v5, /device:TPU:1, one launch (start us, length us, event | category | flops | bytes accessed | tf_op | source)
XLA Modules:
  0.0 35.9 jit_solution(12460863747559414805)
XLA Ops:
  0.6 34.5 %cross_attention.1 = (bf16[128,1024]{1,0:T(8,128)(2,1)S(1)}, bf16[8,512]{1,0:T(8,128)(2,1)S(1)}) custom-call(s32[4]{0:T(128)} %refs_0_.1, s32[4]{0:T(128)} %refs_1_.1, bf16[128,512]{1,0:T(8,128)(2,1)} %refs_2_.1, bf16[128,512]{1,0:T(8,128)(2,1)} %refs_3_.1, bf16[128,512]{1,0:T(8,128)(2,1)} %refs_4_.1, bf16[8,512]{1,0:T(8,128)(2,1)} %refs_5_.1, ...), custom_call_target="tpu_custom_call" | custom-call | tf_op jit(solution)/shard_map/cross_attention/pallas_call | solution.py:397
  35.2 0.7 %write_out.1 = (bf16[128,1024]{1,0:T(8,128)(2,1)}, bf16[8,512]{1,0:T(8,128)(2,1)}) custom-call(bf16[128,1024]{1,0:T(8,128)(2,1)S(1)} %get-tuple-element.4.v_in, bf16[8,512]{1,0:T(8,128)(2,1)S(1)} %get-tuple-element.5.a_in), custom_call_target="tpu_custom_call" | custom-call | tf_op jit(solution)/shard_map/write_out/pallas_call | solution.py:426

commit v6 on v5

--- a/solution.py
+++ b/solution.py
@@ -9,7 +9,7 @@
 
 HEAD_DIM = 64
 NX = 4
-VIDEO = [[[1, 2]], [[3, 0]]]
+VIDEO = [[[2]], [[0, 1], [3]]]
 AUDIO = 2
 MESH = pl.DeviceIdType.MESH
 BF = jnp.bfloat16
@@ -146,6 +146,7 @@
         forbidden = (mark < 4) & (clip_of(audio_pos(m, col >> 5, col & 31), a_end) != mark)
         marks = jnp.where(forbidden, FORBID, 0.0).astype(BF)
         ka[m, 128:256] = jnp.concatenate([marks, marks], axis=1)
+        ka[m, 0:128] = jnp.zeros((128, at), BF)
 
     for i in range(3):
         local[i].wait()
@@ -207,19 +208,19 @@
     mine = jnp.where(c == 0, head0.astype(F32), head1.astype(F32)).astype(BF)
     rest = jnp.where(c == 0, head1.astype(F32), head0.astype(F32)).astype(BF)
     half_at = at // 2
-    upper = lax.broadcasted_iota(jnp.int32, (128, half_at), 0) < 64
 
     def prepare_audio(m):
         rows = pl.ds(pl.multiple_of(m * half_at, half_at), half_at)
-        key = zall[m, :, 0:32].reshape(half_at, 128).astype(F32).T
-        ka[m, 0:128] = jnp.concatenate([jnp.where(upper, key, 0.0), jnp.where(upper, 0.0, key)], axis=1).astype(BF)
+        key = zall[m, :, 0:32].reshape(half_at, 128).T
+        ka[m, 0:64, 0:half_at] = key[0:64]
+        ka[m, 64:128, half_at:at] = key[64:128]
         value = zall[m, :, 32:64].reshape(half_at, 128)
         v0[rows] = value * head0 + head1
         v1[rows] = value * head1 + head0
 
     def prepare_video(m):
         rows = pl.ds(pl.multiple_of(m * (vt // 2), vt // 2), vt // 2)
-        kv[m, 0:128] = kvb[m, :, 0].reshape(vt // 2, 128).astype(F32).T.astype(BF)
+        kv[m, 0:128] = kvb[m, :, 0].reshape(vt // 2, 128).T
         vg[rows] = kvb[m, :, 1].reshape(vt // 2, 128) * mine + rest
 
     prepare_video(c)

time: 36.1 us -> 35.6 us (0.986)
  Pallas kernels: 35.3 us -> 34.8 us
    pallas_call x1, Pallas kernels: 34.5 us -> 34 us  [per_device(): pl.pallas_call(body, out_shape=(pltpu.VMEM((rows, wv.shape[1]), BF), pltp...]
where the time goes in v6:
time: 35.6 us; the launch traced here: 35.4 us
  Pallas kernels  34.8 us (98%)
  between operations  0.64 us (2%)
    pallas_call x1, Pallas kernels, per_device(): pl.pallas_call(body, out_shape=(pltpu.VMEM((rows, wv.shape[1]), BF), pltp...  34 us
    pallas_call x1, Pallas kernels, per_device(): pl.pallas_call(write_out, out_shape=shapes, in_specs=[vmem, vmem], out_sp...  0.72 us

profile of v6, /device:TPU:1, one launch (start us, length us, event | category | flops | bytes accessed | tf_op | source)
XLA Modules:
  0.0 35.4 jit_solution(1108399156053789856)
XLA Ops:
  0.6 34.0 %cross_attention.1 = (bf16[128,1024]{1,0:T(8,128)(2,1)S(1)}, bf16[8,512]{1,0:T(8,128)(2,1)S(1)}) custom-call(s32[4]{0:T(128)} %refs_0_.1, s32[4]{0:T(128)} %refs_1_.1, bf16[128,512]{1,0:T(8,128)(2,1)} %refs_2_.1, bf16[128,512]{1,0:T(8,128)(2,1)} %refs_3_.1, bf16[128,512]{1,0:T(8,128)(2,1)} %refs_4_.1, bf16[8,512]{1,0:T(8,128)(2,1)} %refs_5_.1, ...), custom_call_target="tpu_custom_call" | custom-call | tf_op jit(solution)/shard_map/cross_attention/pallas_call | solution.py:398
  34.7 0.7 %write_out.1 = (bf16[128,1024]{1,0:T(8,128)(2,1)}, bf16[8,512]{1,0:T(8,128)(2,1)}) custom-call(bf16[128,1024]{1,0:T(8,128)(2,1)S(1)} %get-tuple-element.4.v_in, bf16[8,512]{1,0:T(8,128)(2,1)S(1)} %get-tuple-element.5.a_in), custom_call_target="tpu_custom_call" | custom-call | tf_op jit(solution)/shard_map/write_out/pallas_call | solution.py:427
